TPU v7x, 32 devices: a whole 2x2x4 slice. The times are simulated.
32 devices in a mesh: field: 4 (over y, x), shard: 8 (over z, core).
Axes of the slice: x: 2, y: 2, z: 4, core: 2. Of those that a mesh axis runs over, the one named last changes fastest.
Arguments:
- focal_uv: float32 [512, 6, 2, 128], P(('field', 'shard')), may hold values from -1 to 1
- offsets: float32 [512, 6, 2, 128], P(('field', 'shard')), may hold values from -6 to 6
- w_diag: float32 [512, 6, 2, 128], P(('field', 'shard')), may hold values from 0.5 to 8
- w_corr: float32 [512, 6, 128], P(('field', 'shard')), may hold values from -0.6 to 0.6
- star_count: int32 [512], P(('field', 'shard')), may hold values from 16 to 128
- exposure_ids: int32 [512, 6], P(('field', 'shard')), may hold values from 0 to 4095, as said below
- ccd_ids: int32 [512, 6], P(('field', 'shard')), may hold values from 0 to 188
- exp_slot: int32 [4096], replicated, may hold values from 0 to 4095, as said below
Outputs:
- star_update: float32 [512, 2, 128], P(('field', 'shard'))
- exposure_update: float32 [56, 4096], P(None, ('field', 'shard'))
- ccd_update: float32 [189, 6], replicated
Inputs may be any that keep to these rules, and one draw needn't show every extreme that they name: `exposure_ids`: exposure e belongs to owner (exp_slot[e] // 128) % 8 and field block exp_slot[e] // 1024. Among the 96 tile visits of one device (aligned blocks of 16 tiles), at most 16 have exposures of one owner, and exactly 16 for half of the owners; at most 8 have exposures of one owner in one field block, and exactly 8 for some pairs. `exp_slot`: A permutation.
All inputs are finite; a program needn't handle non-finite values.
Results may differ from a plain program's by a relative error of at most 0.0003.
Values sent between devices are 32-bit elements; how exact they have to be, the bound alone decides.
A program may use at most 256 MiB of HBM per device.

v0:
```python
import math

import jax
import jax.numpy as jnp
from jax import lax
from jax.sharding import PartitionSpec as P

ORDER = 6
POLY = 28
NCCD = 189
EXP_DEV = 128


STAR_DAMP = 0.1
EXPOSURE_DAMP = 1.0
DETECTOR_DAMP = 1.0
HIGH = lax.Precision.HIGHEST


def legendre_terms(coord_u, coord_v):

    def series(value):
        values = [jnp.ones_like(value), value]
        for degree in range(1, ORDER):
            values.append(
                ((2 * degree + 1) * value * values[degree] - degree * values[degree - 1])
                / (degree + 1)
            )
        return values

    series_u = series(coord_u)
    series_v = series(coord_v)
    terms = []
    for total in range(ORDER + 1):
        for first in range(total + 1):
            second = total - first
            terms.append(
                math.sqrt((2 * first + 1) * (2 * second + 1)) * series_u[first] * series_v[second]
            )
    return jnp.stack(terms, axis=-2)


def plane_terms(coord_u, coord_v):
    return jnp.stack([jnp.ones_like(coord_u), coord_u, coord_v], axis=-2)


def star_terms(offsets, w_diag, w_corr, star_count):
    stars = offsets.shape[-1]
    present = (jnp.arange(stars, dtype=jnp.int32)[None, :] < star_count[:, None]).astype(
        jnp.float32
    )[:, None, :]
    weight_xx = w_diag[:, :, 0] * present
    weight_yy = w_diag[:, :, 1] * present
    weight_xy = w_corr * jnp.sqrt(w_diag[:, :, 0] * w_diag[:, :, 1]) * present
    resid_x = offsets[:, :, 0]
    resid_y = offsets[:, :, 1]
    hess_xx = jnp.sum(weight_xx, 1) + STAR_DAMP
    hess_yy = jnp.sum(weight_yy, 1) + STAR_DAMP
    hess_xy = jnp.sum(weight_xy, 1)
    determ = hess_xx * hess_yy - hess_xy * hess_xy
    inv_xx = (hess_yy / determ)[:, None]
    inv_yy = (hess_xx / determ)[:, None]
    inv_xy = (-hess_xy / determ)[:, None]
    grad_x = jnp.sum(weight_xx * resid_x + weight_xy * resid_y, 1)[:, None]
    grad_y = jnp.sum(weight_xy * resid_x + weight_yy * resid_y, 1)[:, None]
    left_x = resid_x - (inv_xx * grad_x + inv_xy * grad_y)
    left_y = resid_y - (inv_xy * grad_x + inv_yy * grad_y)
    pull_x = weight_xx * left_x + weight_xy * left_y
    pull_y = weight_xy * left_x + weight_yy * left_y
    prod_11 = inv_xx * weight_xx + inv_xy * weight_xy
    prod_12 = inv_xx * weight_xy + inv_xy * weight_yy
    prod_21 = inv_xy * weight_xx + inv_yy * weight_xy
    prod_22 = inv_xy * weight_xy + inv_yy * weight_yy
    schur_xx = weight_xx - (weight_xx * prod_11 + weight_xy * prod_21)
    schur_yy = weight_yy - (weight_xy * prod_12 + weight_yy * prod_22)
    schur_xy = weight_xy - (weight_xx * prod_12 + weight_xy * prod_22)
    return (
        (inv_xx, inv_yy, inv_xy),
        (weight_xx, weight_yy, weight_xy),
        (schur_xx, schur_yy, schur_xy, pull_x, pull_y),
    )


def normal_vectors(basis, schur_xx, schur_yy, schur_xy, pull_x, pull_y):

    def outer(scale):
        product = jnp.einsum(
            "...ps,...qs->...pq", basis * scale[..., None, :], basis, precision=HIGH
        )
        return product.reshape(scale.shape[:-1] + (-1,))

    grad_x = jnp.einsum("...ps,...s->...p", basis, pull_x, precision=HIGH)
    grad_y = jnp.einsum("...ps,...s->...p", basis, pull_y, precision=HIGH)
    return jnp.concatenate(
        [outer(schur_xx), outer(schur_yy), outer(schur_xy), grad_x, grad_y], axis=-1
    )


def batched_cholesky_solve(matrix, rhs):
    order_n = matrix.shape[0]
    rows_idx = jnp.arange(order_n, dtype=jnp.int32)
    work = matrix
    columns = []
    for step in range(order_n):
        pivot = jnp.sqrt(work[step, step])
        column = work[:, step] / pivot[None, :]
        column = jnp.where((rows_idx >= step)[:, None], column, jnp.float32(0.0))
        columns.append(column)
        work = work - column[:, None, :] * column[None, :, :]
    lower = jnp.stack(columns, axis=1)
    remain = rhs
    forward = []
    for step in range(order_n):
        value = remain[step] / lower[step, step]
        forward.append(value)
        remain = remain - lower[:, step] * value[None, :]
    remain = jnp.stack(forward, axis=0)
    backward = [None] * order_n
    for step in range(order_n - 1, -1, -1):
        value = remain[step] / lower[step, step]
        backward[step] = value
        remain = remain - lower[step] * value[None, :]
    return jnp.stack(backward, axis=0)


def solve_blocks(vectors, width, damping):
    square = width * width
    flipped = vectors.T
    count = vectors.shape[0]
    part_xx = flipped[:square].reshape(width, width, count)
    part_yy = flipped[square : 2 * square].reshape(width, width, count)
    part_xy = flipped[2 * square : 3 * square].reshape(width, width, count)
    matrix = jnp.concatenate(
        [jnp.concatenate([part_xx, part_xy], 1), jnp.concatenate([part_xy, part_yy], 1)], 0
    )
    matrix = matrix + damping * jnp.eye(2 * width, dtype=jnp.float32)[:, :, None]
    rhs = flipped[3 * square : 3 * square + 2 * width]
    return batched_cholesky_solve(matrix, rhs).T


def star_solve(inverse, weights, offsets, model_x, model_y):
    inv_xx, inv_yy, inv_xy = inverse
    weight_xx, weight_yy, weight_xy = weights
    left_x = offsets[:, :, 0] - model_x
    left_y = offsets[:, :, 1] - model_y
    grad_x = jnp.sum(weight_xx * left_x + weight_xy * left_y, 1)
    grad_y = jnp.sum(weight_xy * left_x + weight_yy * left_y, 1)
    return jnp.stack(
        [
            inv_xx[:, 0] * grad_x + inv_xy[:, 0] * grad_y,
            inv_xy[:, 0] * grad_x + inv_yy[:, 0] * grad_y,
        ],
        axis=1,
    )


def shards(focal_uv, offsets, w_diag, w_corr, star_count, exposure_ids, ccd_ids, exp_slot):
    shard_count = lax.axis_size("shard")
    field_count = lax.axis_size("field")
    tiles = offsets.shape[0]
    visits = offsets.shape[1]
    visits_all = tiles * visits
    capacity = 4 * visits_all // (3 * shard_count)
    slot_total = shard_count * capacity
    exp_local = EXP_DEV
    sentinel = field_count * exp_local
    vec_width = 3 * POLY * POLY + 2 * POLY
    padded_width = (vec_width + 128) // 128 * 128
    terms = star_terms(offsets, w_diag, w_corr, star_count)
    reduced = terms[2]
    coord_u = focal_uv[:, :, 0]
    coord_v = focal_uv[:, :, 1]
    basis = legendre_terms(coord_u, coord_v)
    plane = plane_terms(coord_u, coord_v)
    ccd_vec = normal_vectors(plane, *reduced).reshape(visits_all, -1)
    ccd_local = jax.ops.segment_sum(ccd_vec, ccd_ids.reshape(-1), num_segments=NCCD)
    ccd_table = lax.psum(ccd_local, ("field", "shard"))
    ccd_update = solve_blocks(ccd_table, 3, DETECTOR_DAMP)
    position = exp_slot[exposure_ids.reshape(-1)]
    owner = position // exp_local % shard_count
    row_index = position // (exp_local * shard_count) * exp_local + position % exp_local
    one_hot = (owner[:, None] == jnp.arange(shard_count, dtype=jnp.int32)[None, :]).astype(
        jnp.int32
    )
    earlier = jnp.cumsum(one_hot, axis=0) - one_hot
    target = owner * capacity + jnp.sum(earlier * one_hot, axis=1)
    local = normal_vectors(basis, *reduced).reshape(visits_all, vec_width)
    payload = jnp.concatenate(
        [
            local,
            row_index.astype(jnp.float32)[:, None],
            jnp.zeros((visits_all, padded_width - vec_width - 1), jnp.float32),
        ],
        axis=1,
    )
    outgoing = (
        jnp.zeros((slot_total, padded_width), jnp.float32)
        .at[:, vec_width]
        .set(float(sentinel))
        .at[target]
        .set(payload)
    )
    carried = lax.all_to_all(outgoing, "shard", split_axis=0, concat_axis=0, tiled=True)
    arrived_rows = carried[:, vec_width].astype(jnp.int32)
    table = jax.ops.segment_sum(carried, arrived_rows, num_segments=sentinel + 1)[:sentinel]
    summed = lax.psum_scatter(table, "field", scatter_dimension=0, tiled=True)
    solution = solve_blocks(summed[:, :vec_width], POLY, EXPOSURE_DAMP)
    exposure_update = solution.T
    column_table = lax.all_gather(exposure_update, "field", axis=1, tiled=True)
    column_table = jnp.concatenate([column_table, jnp.zeros((2 * POLY, 1), jnp.float32)], axis=1)
    looked_up = column_table[:, arrived_rows]
    returned = lax.all_to_all(looked_up, "shard", split_axis=1, concat_axis=1, tiled=True)
    coeff = returned[:, target].T
    coeff = coeff.reshape(tiles, visits, 2 * POLY)
    det_coeff = ccd_update[ccd_ids]
    model_x = jnp.einsum("tkp,tkps->tks", coeff[..., :POLY], basis, precision=HIGH) + jnp.einsum(
        "tkp,tkps->tks", det_coeff[..., :3], plane, precision=HIGH
    )
    model_y = jnp.einsum("tkp,tkps->tks", coeff[..., POLY:], basis, precision=HIGH) + jnp.einsum(
        "tkp,tkps->tks", det_coeff[..., 3:], plane, precision=HIGH
    )
    star_update = star_solve(terms[0], terms[1], offsets, model_x, model_y)
    return (star_update, exposure_update, ccd_update)


def solution(mesh):
    in_specs = (
        P(("field", "shard"), None, None, None),
        P(("field", "shard"), None, None, None),
        P(("field", "shard"), None, None, None),
        P(("field", "shard"), None, None),
        P(("field", "shard")),
        P(("field", "shard"), None),
        P(("field", "shard"), None),
        P(),
    )
    out_specs = (P(("field", "shard"), None, None), P(None, ("field", "shard")), P())
    return jax.shard_map(shards, mesh=mesh, in_specs=in_specs, out_specs=out_specs, check_vma=False)
```

profile of v0, /device:TPU:0, one launch (start us, length us, event | category | flops | bytes accessed | tf_op | source)
XLA Modules:
  0.0 718.1 jit_solution(4685828884842313147)
XLA Ops:
  34.4 6.1 fusion.4
  57.1 6.5 all-to-all-start
  70.8 44.1 %psum.7 = f32[33,189]{1,0:T(8,128)S(1)} all-reduce(f32[33,189]{1,0:T(8,128)S(1)} %bitcast.1311), channel_id=1, replica_groups=mesh['field'=4,'shard'=8] {'field','shard'}, use_global_device_ids=true, to_apply=%region_12.13 | all-reduce | flops 6237 | bytes 49896 | tf_op jit(solution)/shard_map/psum | solution.py:177
  127.3 6.2 copy.1072
  153.7 39.1 %reduce-scatter.2.cloned.1.call-done = f32[128,2432]{0,1:T(8,128)} async-done(((f32[512,2432]{0,1:T(8,128)}), f32[128,2432]{0,1:T(8,128)}) %reduce-scatter.2.cloned.1.call-update) | async-done | bytes 1245200 | tf_op jit(solution)/shard_map/reduce_scatter | solution.py:206
  320.4 5.1 multiply_subtract_fusion.22
  327.4 5.0 multiply_subtract_fusion.21
  334.3 5.4 multiply_subtract_fusion.20
  341.5 5.8 multiply_subtract_fusion.19
  349.2 10.4 %multiply_subtract_fusion.18 = f32[56,56,128]{2,0,1:T(8,128)S(1)} fusion(f32[56,128]{1,0:T(8,128)S(1)} %fusion.175, f32[56,128]{1,0:T(8,128)S(1)} %fusion.336, f32[56,128]{1,0:T(8,128)S(1)} %fusion.176, f32[56,128]{1,0:T(8,128)S(1)} %fusion.337, f32[56,128]{1,0:T(8,128)S(1)} %fusion.177, f32[56,128]{1,0:T(8,128)S(1)} %fusion.338, f32[56,128]{1,0:T(8,128)S(1)} %fusion.178, ...), kind=kLoop, calls=%fused_computation.29 | loop fusion | flops 30105600 | bytes 5345536 | tf_op jit(solution)/shard_map/sub | solution.py:109
  361.6 10.8 %multiply_subtract_fusion.17 = f32[56,56,128]{2,0,1:T(8,128)S(1)} fusion(f32[56,128]{1,0:T(8,128)S(1)} %fusion.174, f32[56,128]{1,0:T(8,128)S(1)} %fusion.335, f32[56,128]{1,0:T(8,128)S(1)} %fusion.175, f32[56,128]{1,0:T(8,128)S(1)} %fusion.336, f32[56,128]{1,0:T(8,128)S(1)} %fusion.176, f32[56,128]{1,0:T(8,128)S(1)} %fusion.337, f32[56,128]{1,0:T(8,128)S(1)} %fusion.177, ...), kind=kLoop, calls=%fused_computation.28 | loop fusion | flops 30908416 | bytes 5402880 | tf_op jit(solution)/shard_map/sub | solution.py:109
  374.2 11.4 %multiply_subtract_fusion.16 = f32[56,56,128]{2,0,1:T(8,128)S(1)} fusion(f32[56,128]{1,0:T(8,128)S(1)} %fusion.173, f32[56,128]{1,0:T(8,128)S(1)} %fusion.334, f32[56,128]{1,0:T(8,128)S(1)} %fusion.174, f32[56,128]{1,0:T(8,128)S(1)} %fusion.335, f32[56,128]{1,0:T(8,128)S(1)} %fusion.175, f32[56,128]{1,0:T(8,128)S(1)} %fusion.336, f32[56,128]{1,0:T(8,128)S(1)} %fusion.176, ...), kind=kLoop, calls=%fused_computation.27 | loop fusion | flops 31711232 | bytes 5460224 | tf_op jit(solution)/shard_map/sub | solution.py:109
  387.5 11.3 %multiply_subtract_fusion.15 = f32[56,56,128]{2,0,1:T(8,128)S(1)} fusion(f32[56,128]{1,0:T(8,128)S(1)} %fusion.172, f32[56,128]{1,0:T(8,128)S(1)} %fusion.333, f32[56,128]{1,0:T(8,128)S(1)} %fusion.173, f32[56,128]{1,0:T(8,128)S(1)} %fusion.334, f32[56,128]{1,0:T(8,128)S(1)} %fusion.174, f32[56,128]{1,0:T(8,128)S(1)} %fusion.335, f32[56,128]{1,0:T(8,128)S(1)} %fusion.175, ...), kind=kLoop, calls=%fused_computation.26 | loop fusion | flops 32514048 | bytes 5517568 | tf_op jit(solution)/shard_map/sub | solution.py:109
  400.7 11.7 %multiply_subtract_fusion.14 = f32[56,56,128]{2,0,1:T(8,128)S(1)} fusion(f32[56,128]{1,0:T(8,128)S(1)} %fusion.171, f32[56,128]{1,0:T(8,128)S(1)} %fusion.332, f32[56,128]{1,0:T(8,128)S(1)} %fusion.172, f32[56,128]{1,0:T(8,128)S(1)} %fusion.333, f32[56,128]{1,0:T(8,128)S(1)} %fusion.173, f32[56,128]{1,0:T(8,128)S(1)} %fusion.334, f32[56,128]{1,0:T(8,128)S(1)} %fusion.174, ...), kind=kLoop, calls=%fused_computation.25 | loop fusion | flops 33316864 | bytes 5574912 | tf_op jit(solution)/shard_map/sub | solution.py:109
  414.3 12.1 %multiply_subtract_fusion.13 = f32[56,56,128]{2,0,1:T(8,128)S(1)} fusion(f32[56,128]{1,0:T(8,128)S(1)} %fusion.170, f32[56,128]{1,0:T(8,128)S(1)} %fusion.331, f32[56,128]{1,0:T(8,128)S(1)} %fusion.171, f32[56,128]{1,0:T(8,128)S(1)} %fusion.332, f32[56,128]{1,0:T(8,128)S(1)} %fusion.172, f32[56,128]{1,0:T(8,128)S(1)} %fusion.333, f32[56,128]{1,0:T(8,128)S(1)} %fusion.173, ...), kind=kLoop, calls=%fused_computation.24 | loop fusion | flops 34119680 | bytes 5632256 | tf_op jit(solution)/shard_map/sub | solution.py:109
  428.3 12.2 %multiply_subtract_fusion.12 = f32[56,56,128]{2,0,1:T(8,128)S(1)} fusion(f32[56,128]{1,0:T(8,128)S(1)} %fusion.169, f32[56,128]{1,0:T(8,128)S(1)} %fusion.330, f32[56,128]{1,0:T(8,128)S(1)} %fusion.170, f32[56,128]{1,0:T(8,128)S(1)} %fusion.331, f32[56,128]{1,0:T(8,128)S(1)} %fusion.171, f32[56,128]{1,0:T(8,128)S(1)} %fusion.332, f32[56,128]{1,0:T(8,128)S(1)} %fusion.172, ...), kind=kLoop, calls=%fused_computation.23 | loop fusion | flops 34922496 | bytes 5689600 | tf_op jit(solution)/shard_map/sub | solution.py:109
  442.4 12.5 %multiply_subtract_fusion.11 = f32[56,56,128]{2,0,1:T(8,128)S(1)} fusion(f32[56,128]{1,0:T(8,128)S(1)} %fusion.168, f32[56,128]{1,0:T(8,128)S(1)} %fusion.329, f32[56,128]{1,0:T(8,128)S(1)} %fusion.169, f32[56,128]{1,0:T(8,128)S(1)} %fusion.330, f32[56,128]{1,0:T(8,128)S(1)} %fusion.170, f32[56,128]{1,0:T(8,128)S(1)} %fusion.331, f32[56,128]{1,0:T(8,128)S(1)} %fusion.171, ...), kind=kLoop, calls=%fused_computation.22 | loop fusion | flops 35725312 | bytes 5746944 | tf_op jit(solution)/shard_map/sub | solution.py:109
  456.7 13.0 %multiply_subtract_fusion.10 = f32[56,56,128]{2,0,1:T(8,128)S(1)} fusion(f32[56,128]{1,0:T(8,128)S(1)} %fusion.167, f32[56,128]{1,0:T(8,128)S(1)} %fusion.328, f32[56,128]{1,0:T(8,128)S(1)} %fusion.168, f32[56,128]{1,0:T(8,128)S(1)} %fusion.329, f32[56,128]{1,0:T(8,128)S(1)} %fusion.169, f32[56,128]{1,0:T(8,128)S(1)} %fusion.330, f32[56,128]{1,0:T(8,128)S(1)} %fusion.170, ...), kind=kLoop, calls=%fused_computation.21 | loop fusion | flops 36528128 | bytes 5804288 | tf_op jit(solution)/shard_map/sub | solution.py:109
  471.6 13.1 %multiply_subtract_fusion.9 = f32[56,56,128]{2,0,1:T(8,128)S(1)} fusion(f32[56,128]{1,0:T(8,128)S(1)} %fusion.166, f32[56,128]{1,0:T(8,128)S(1)} %fusion.327, f32[56,128]{1,0:T(8,128)S(1)} %fusion.167, f32[56,128]{1,0:T(8,128)S(1)} %fusion.328, f32[56,128]{1,0:T(8,128)S(1)} %fusion.168, f32[56,128]{1,0:T(8,128)S(1)} %fusion.329, f32[56,128]{1,0:T(8,128)S(1)} %fusion.169, ...), kind=kLoop, calls=%fused_computation.20 | loop fusion | flops 37330944 | bytes 5861632 | tf_op jit(solution)/shard_map/sub | solution.py:109
  485.9 13.3 %multiply_subtract_fusion.8 = f32[56,56,128]{2,0,1:T(8,128)S(1)} fusion(f32[56,128]{1,0:T(8,128)S(1)} %fusion.165, f32[56,128]{1,0:T(8,128)S(1)} %fusion.326, f32[56,128]{1,0:T(8,128)S(1)} %fusion.166, f32[56,128]{1,0:T(8,128)S(1)} %fusion.327, f32[56,128]{1,0:T(8,128)S(1)} %fusion.167, f32[56,128]{1,0:T(8,128)S(1)} %fusion.328, f32[56,128]{1,0:T(8,128)S(1)} %fusion.168, ...), kind=kLoop, calls=%fused_computation.19 | loop fusion | flops 38133760 | bytes 5918976 | tf_op jit(solution)/shard_map/sub | solution.py:109
  500.1 14.1 %multiply_subtract_fusion.7 = f32[56,56,128]{2,0,1:T(8,128)S(1)} fusion(f32[56,128]{1,0:T(8,128)S(1)} %fusion.164, f32[56,128]{1,0:T(8,128)S(1)} %fusion.325, f32[56,128]{1,0:T(8,128)S(1)} %fusion.165, f32[56,128]{1,0:T(8,128)S(1)} %fusion.326, f32[56,128]{1,0:T(8,128)S(1)} %fusion.166, f32[56,128]{1,0:T(8,128)S(1)} %fusion.327, f32[56,128]{1,0:T(8,128)S(1)} %fusion.167, ...), kind=kLoop, calls=%fused_computation.18 | loop fusion | flops 38936576 | bytes 5976320 | tf_op jit(solution)/shard_map/sub | solution.py:109
  515.0 14.1 %multiply_subtract_fusion.6 = f32[56,56,128]{2,0,1:T(8,128)S(1)} fusion(f32[56,128]{1,0:T(8,128)S(1)} %fusion.163, f32[56,128]{1,0:T(8,128)S(1)} %fusion.324, f32[56,128]{1,0:T(8,128)S(1)} %fusion.164, f32[56,128]{1,0:T(8,128)S(1)} %fusion.325, f32[56,128]{1,0:T(8,128)S(1)} %fusion.165, f32[56,128]{1,0:T(8,128)S(1)} %fusion.326, f32[56,128]{1,0:T(8,128)S(1)} %fusion.166, ...), kind=kLoop, calls=%fused_computation.17 | loop fusion | flops 39739392 | bytes 6033664 | tf_op jit(solution)/shard_map/sub | solution.py:109
  530.0 14.5 %multiply_subtract_fusion.5 = f32[56,56,128]{2,0,1:T(8,128)S(1)} fusion(f32[56,128]{1,0:T(8,128)S(1)} %fusion.162, f32[56,128]{1,0:T(8,128)S(1)} %fusion.323, f32[56,128]{1,0:T(8,128)S(1)} %fusion.163, f32[56,128]{1,0:T(8,128)S(1)} %fusion.324, f32[56,128]{1,0:T(8,128)S(1)} %fusion.164, f32[56,128]{1,0:T(8,128)S(1)} %fusion.325, f32[56,128]{1,0:T(8,128)S(1)} %fusion.165, ...), kind=kLoop, calls=%fused_computation.16 | loop fusion | flops 40542208 | bytes 6091008 | tf_op jit(solution)/shard_map/sub | solution.py:109
  545.6 9.3 %multiply_subtract_fusion.4 = f32[56,56,128]{2,0,1:T(8,128)S(1)} fusion(f32[56,128]{1,0:T(8,128)S(1)} %fusion.161, f32[56,128]{1,0:T(8,128)S(1)} %fusion.322, f32[56,128]{1,0:T(8,128)S(1)} %fusion.162, f32[56,128]{1,0:T(8,128)S(1)} %fusion.323, f32[56,128]{1,0:T(8,128)S(1)} %fusion.163, f32[56,128]{1,0:T(8,128)S(1)} %fusion.324, f32[56,128]{1,0:T(8,128)S(1)} %fusion.164, ...), kind=kLoop, calls=%fused_computation.15 | loop fusion | flops 41345024 | bytes 6148352 | tf_op jit(solution)/shard_map/sub | solution.py:109
  555.8 9.9 %multiply_subtract_fusion.3 = f32[56,56,128]{2,0,1:T(8,128)S(1)} fusion(f32[56,128]{1,0:T(8,128)S(1)} %fusion.160, f32[56,128]{1,0:T(8,128)S(1)} %fusion.321, f32[56,128]{1,0:T(8,128)S(1)} %fusion.161, f32[56,128]{1,0:T(8,128)S(1)} %fusion.322, f32[56,128]{1,0:T(8,128)S(1)} %fusion.162, f32[56,128]{1,0:T(8,128)S(1)} %fusion.323, f32[56,128]{1,0:T(8,128)S(1)} %fusion.163, ...), kind=kLoop, calls=%fused_computation.14 | loop fusion | flops 42147840 | bytes 6205696 | tf_op jit(solution)/shard_map/sub | solution.py:109
  566.6 10.7 %multiply_subtract_fusion.2 = f32[56,56,128]{2,0,1:T(8,128)S(1)} fusion(f32[56,128]{1,0:T(8,128)S(1)} %fusion.159, f32[56,128]{1,0:T(8,128)S(1)} %fusion.320, f32[56,128]{1,0:T(8,128)S(1)} %fusion.160, f32[56,128]{1,0:T(8,128)S(1)} %fusion.321, f32[56,128]{1,0:T(8,128)S(1)} %fusion.161, f32[56,128]{1,0:T(8,128)S(1)} %fusion.322, f32[56,128]{1,0:T(8,128)S(1)} %fusion.162, ...), kind=kLoop, calls=%fused_computation.13 | loop fusion | flops 42950656 | bytes 6263040 | tf_op jit(solution)/shard_map/sub | solution.py:109
  578.3 13.4 %multiply_subtract_fusion.1 = f32[56,56,128]{2,0,1:T(8,128)} fusion(f32[56,128]{1,0:T(8,128)S(1)} %fusion.158, f32[56,128]{1,0:T(8,128)S(1)} %fusion.319, f32[56,128]{1,0:T(8,128)S(1)} %fusion.159, f32[56,128]{1,0:T(8,128)S(1)} %fusion.320, f32[56,128]{1,0:T(8,128)S(1)} %fusion.160, f32[56,128]{1,0:T(8,128)S(1)} %fusion.321, f32[56,128]{1,0:T(8,128)S(1)} %fusion.161, ...), kind=kLoop, calls=%fused_computation.12 | loop fusion | flops 43753472 | bytes 6320384 | tf_op jit(solution)/shard_map/sub | solution.py:109
  633.6 11.0 %multiply_subtract_fusion = f32[56,56,128]{2,0,1:T(8,128)S(1)} fusion(f32[56,128]{1,0:T(8,128)S(1)} %fusion.157, f32[56,128]{1,0:T(8,128)S(1)} %fusion.318, f32[56,128]{1,0:T(8,128)S(1)} %fusion.158, f32[56,128]{1,0:T(8,128)S(1)} %fusion.319, f32[56,128]{1,0:T(8,128)S(1)} %fusion.159, f32[56,128]{1,0:T(8,128)S(1)} %fusion.320, f32[56,128]{1,0:T(8,128)S(1)} %fusion.160, ...), kind=kLoop, calls=%fused_computation.11 | loop fusion | flops 44556288 | bytes 6377728 | tf_op jit(solution)/shard_map/sub | solution.py:109
  646.2 9.1 %stack.20 = f32[56,128]{1,0:T(8,128)} concatenate(f32[1,128]{1,0:T(1,128)} %slice_divide_fusion.121, f32[1,128]{1,0:T(1,128)S(1)} %copy-done.146, f32[1,128]{1,0:T(1,128)S(1)} %copy-done.148, f32[1,128]{1,0:T(1,128)S(1)} %copy-done.150, f32[1,128]{1,0:T(1,128)S(1)} %copy-done.152, f32[1,128]{1,0:T(1,128)} %copy-done.153, f32[1,128]{1,0:T(1,128)} %copy-done.154, ...), dimensions={0} | concatenate | bytes 57344 | tf_op jit(solution)/shard_map/stack | solution.py:117
  655.3 12.2 %stack.21 = f32[56,56,128]{2,1,0:T(8,128)} concatenate(f32[56,1,128]{2,1,0:T(1,128)} %bitcast.1367, f32[56,1,128]{2,1,0:T(1,128)S(1)} %bitcast.1313, f32[56,1,128]{2,1,0:T(1,128)S(1)} %bitcast.1314, f32[56,1,128]{2,1,0:T(1,128)S(1)} %bitcast.1315, f32[56,1,128]{2,1,0:T(1,128)S(1)} %bitcast.1316, f32[56,1,128]{2,1,0:T(1,128)S(1)} %bitcast.1317, f32[56,1,128]{2,1,0:T(1,128)S(1)} %bitcast.1318, ...), dimensions={1} | concatenate | bytes 3211264 | tf_op jit(solution)/shard_map/stack | solution.py:110
  683.4 8.7 %all_gather.3 = f32[56,512]{1,0:T(8,128)S(1)} all-gather(f32[56,128]{1,0:T(8,128)S(1)} %stack.22), channel_id=1, replica_groups=mesh['field'=4,'shard'=8] {'field'}, dimensions={1}, use_global_device_ids=true | all-gather | bytes 143360 | tf_op jit(solution)/shard_map/all_gather | solution.py:209
  698.7 5.6 all-to-all-done.1
  (1144 shorter events, 309.8 us)
Async XLA Ops:
  57.1 60.2 %all-to-all-start = ((f32[8,16,2432]{2,1,0:T(8,128)}), f32[8,16,2432]{2,1,0:T(8,128)S(1)}, u32[]{:S(2)}, u32[]{:S(2)}) async-start(f32[8,16,2432]{2,1,0:T(8,128)} %bitcast.17), calls=%async_computation | async-start | bytes 2490368 | tf_op jit(solution)/shard_map/all_to_all | solution.py:203
  63.6 129.2 %reduce-scatter.2.cloned.1.call-start = ((), (), s32[]{:S(2)}) async-start(), calls=%async_computation.3 | async-start | bytes 6225920 | tf_op jit(solution)/shard_map/reduce_scatter | solution.py:206
  135.4 58.8 %copy-start.65 = (f32[6,189]{1,0:T(8,128)}, f32[6,189]{1,0:T(8,128)S(1)}, u32[]{:S(2)}) copy-start(f32[6,189]{1,0:T(8,128)S(1)} %stack.26) | copy-start | bytes 13612
  136.8 67.2 %copy-start.140 = (pred[56]{0:T(512)(128)(4,1)}, pred[56]{0:T(512)(128)(4,1)S(1)}, u32[]{:S(2)}) copy-start(pred[56]{0:T(512)(128)(4,1)S(1)} %iota_compare_fusion.63) | copy-start | bytes 172
  136.8 68.3 %copy-start.138 = (pred[56]{0:T(512)(128)(4,1)}, pred[56]{0:T(512)(128)(4,1)S(1)}, u32[]{:S(2)}) copy-start(pred[56]{0:T(512)(128)(4,1)S(1)} %iota_compare_fusion.62) | copy-start | bytes 172
  136.8 69.2 %copy-start.136 = (pred[56]{0:T(512)(128)(4,1)}, pred[56]{0:T(512)(128)(4,1)S(1)}, u32[]{:S(2)}) copy-start(pred[56]{0:T(512)(128)(4,1)S(1)} %iota_compare_fusion.61) | copy-start | bytes 172
  136.8 71.3 %copy-start.134 = (pred[56]{0:T(512)(128)(4,1)}, pred[56]{0:T(512)(128)(4,1)S(1)}, u32[]{:S(2)}) copy-start(pred[56]{0:T(512)(128)(4,1)S(1)} %iota_compare_fusion.60) | copy-start | bytes 172
  136.8 73.3 %copy-start.132 = (pred[56]{0:T(512)(128)(4,1)}, pred[56]{0:T(512)(128)(4,1)S(1)}, u32[]{:S(2)}) copy-start(pred[56]{0:T(512)(128)(4,1)S(1)} %iota_compare_fusion.59) | copy-start | bytes 172
  136.9 75.5 %copy-start.130 = (pred[56]{0:T(512)(128)(4,1)}, pred[56]{0:T(512)(128)(4,1)S(1)}, u32[]{:S(2)}) copy-start(pred[56]{0:T(512)(128)(4,1)S(1)} %iota_compare_fusion.58) | copy-start | bytes 172
  136.9 77.8 %copy-start.128 = (pred[56]{0:T(512)(128)(4,1)}, pred[56]{0:T(512)(128)(4,1)S(1)}, u32[]{:S(2)}) copy-start(pred[56]{0:T(512)(128)(4,1)S(1)} %iota_compare_fusion.57) | copy-start | bytes 172
  136.9 80.1 %copy-start.126 = (pred[56]{0:T(512)(128)(4,1)}, pred[56]{0:T(512)(128)(4,1)S(1)}, u32[]{:S(2)}) copy-start(pred[56]{0:T(512)(128)(4,1)S(1)} %iota_compare_fusion.56) | copy-start | bytes 172
  136.9 82.8 %copy-start.124 = (pred[56]{0:T(512)(128)(4,1)}, pred[56]{0:T(512)(128)(4,1)S(1)}, u32[]{:S(2)}) copy-start(pred[56]{0:T(512)(128)(4,1)S(1)} %iota_compare_fusion.55) | copy-start | bytes 172
  136.9 85.3 %copy-start.122 = (pred[56]{0:T(512)(128)(4,1)}, pred[56]{0:T(512)(128)(4,1)S(1)}, u32[]{:S(2)}) copy-start(pred[56]{0:T(512)(128)(4,1)S(1)} %iota_compare_fusion.54) | copy-start | bytes 172
  137.0 88.0 %copy-start.120 = (pred[56]{0:T(512)(128)(4,1)}, pred[56]{0:T(512)(128)(4,1)S(1)}, u32[]{:S(2)}) copy-start(pred[56]{0:T(512)(128)(4,1)S(1)} %iota_compare_fusion.53) | copy-start | bytes 172
  137.0 90.8 %copy-start.118 = (pred[56]{0:T(512)(128)(4,1)}, pred[56]{0:T(512)(128)(4,1)S(1)}, u32[]{:S(2)}) copy-start(pred[56]{0:T(512)(128)(4,1)S(1)} %iota_compare_fusion.52) | copy-start | bytes 172
  137.0 93.7 %copy-start.116 = (pred[56]{0:T(512)(128)(4,1)}, pred[56]{0:T(512)(128)(4,1)S(1)}, u32[]{:S(2)}) copy-start(pred[56]{0:T(512)(128)(4,1)S(1)} %iota_compare_fusion.51) | copy-start | bytes 172
  137.0 96.7 %copy-start.114 = (pred[56]{0:T(512)(128)(4,1)}, pred[56]{0:T(512)(128)(4,1)S(1)}, u32[]{:S(2)}) copy-start(pred[56]{0:T(512)(128)(4,1)S(1)} %iota_compare_fusion.50) | copy-start | bytes 172
  137.1 99.7 %copy-start.112 = (pred[56]{0:T(512)(128)(4,1)}, pred[56]{0:T(512)(128)(4,1)S(1)}, u32[]{:S(2)}) copy-start(pred[56]{0:T(512)(128)(4,1)S(1)} %iota_compare_fusion.49) | copy-start | bytes 172
  137.1 103.2 %copy-start.110 = (pred[56]{0:T(512)(128)(4,1)}, pred[56]{0:T(512)(128)(4,1)S(1)}, u32[]{:S(2)}) copy-start(pred[56]{0:T(512)(128)(4,1)S(1)} %iota_compare_fusion.48) | copy-start | bytes 172
  137.1 107.2 %copy-start.108 = (pred[56]{0:T(512)(128)(4,1)}, pred[56]{0:T(512)(128)(4,1)S(1)}, u32[]{:S(2)}) copy-start(pred[56]{0:T(512)(128)(4,1)S(1)} %iota_compare_fusion.47) | copy-start | bytes 172
  137.1 110.6 %copy-start.106 = (pred[56]{0:T(512)(128)(4,1)}, pred[56]{0:T(512)(128)(4,1)S(1)}, u32[]{:S(2)}) copy-start(pred[56]{0:T(512)(128)(4,1)S(1)} %iota_compare_fusion.46) | copy-start | bytes 172
  137.1 113.8 %copy-start.104 = (pred[56]{0:T(512)(128)(4,1)}, pred[56]{0:T(512)(128)(4,1)S(1)}, u32[]{:S(2)}) copy-start(pred[56]{0:T(512)(128)(4,1)S(1)} %iota_compare_fusion.45) | copy-start | bytes 172
  137.2 117.2 %copy-start.102 = (pred[56]{0:T(512)(128)(4,1)}, pred[56]{0:T(512)(128)(4,1)S(1)}, u32[]{:S(2)}) copy-start(pred[56]{0:T(512)(128)(4,1)S(1)} %iota_compare_fusion.44) | copy-start | bytes 172
  137.2 121.1 %copy-start.100 = (pred[56]{0:T(512)(128)(4,1)}, pred[56]{0:T(512)(128)(4,1)S(1)}, u32[]{:S(2)}) copy-start(pred[56]{0:T(512)(128)(4,1)S(1)} %iota_compare_fusion.43) | copy-start | bytes 172
  137.2 124.8 %copy-start.98 = (pred[56]{0:T(512)(128)(4,1)}, pred[56]{0:T(512)(128)(4,1)S(1)}, u32[]{:S(2)}) copy-start(pred[56]{0:T(512)(128)(4,1)S(1)} %iota_compare_fusion.42) | copy-start | bytes 172
  137.2 128.6 %copy-start.96 = (pred[56]{0:T(512)(128)(4,1)}, pred[56]{0:T(512)(128)(4,1)S(1)}, u32[]{:S(2)}) copy-start(pred[56]{0:T(512)(128)(4,1)S(1)} %iota_compare_fusion.41) | copy-start | bytes 172
  137.3 133.5 %copy-start.94 = (pred[56]{0:T(512)(128)(4,1)}, pred[56]{0:T(512)(128)(4,1)S(1)}, u32[]{:S(2)}) copy-start(pred[56]{0:T(512)(128)(4,1)S(1)} %iota_compare_fusion.40) | copy-start | bytes 172
  137.3 139.0 %copy-start.92 = (pred[56]{0:T(512)(128)(4,1)}, pred[56]{0:T(512)(128)(4,1)S(1)}, u32[]{:S(2)}) copy-start(pred[56]{0:T(512)(128)(4,1)S(1)} %iota_compare_fusion.39) | copy-start | bytes 172
  610.4 34.2 %copy-start.167 = (f32[1,128]{1,0:T(1,128)}, f32[1,128]{1,0:T(1,128)S(1)}, u32[]{:S(2)}) copy-start(f32[1,128]{1,0:T(1,128)S(1)} %slice_divide_fusion.102) | copy-start | bytes 1540
  610.5 34.1 %copy-start.168 = (f32[1,128]{1,0:T(1,128)}, f32[1,128]{1,0:T(1,128)S(1)}, u32[]{:S(2)}) copy-start(f32[1,128]{1,0:T(1,128)S(1)} %slice_divide_fusion.101) | copy-start | bytes 1540
  610.6 34.0 %copy-start.169 = (f32[1,128]{1,0:T(1,128)}, f32[1,128]{1,0:T(1,128)S(1)}, u32[]{:S(2)}) copy-start(f32[1,128]{1,0:T(1,128)S(1)} %slice_divide_fusion.100) | copy-start | bytes 1540
  693.8 10.6 %all-to-all-start.1 = ((f32[8,1,896]{2,1,0:T(1,128)}), f32[8,1,896]{2,1,0:T(1,128)S(1)}, u32[]{:S(2)}, u32[]{:S(2)}) async-start(f32[8,1,896]{2,1,0:T(1,128)} %reshape.3919), calls=%async_computation.2 | async-start | bytes 57344 | tf_op jit(solution)/shard_map/all_to_all | solution.py:212
  (176 other events, 2205.1 us)
Sparse Core Ops, SparseCore 0:
  133.7 59.0 reduce-scatter.1
where the time goes:
time: 733 us; the launch traced here: 718 us
  other arithmetic  450 us (61%)
  local copies, waits for them, and re-layouts  108 us (15%)
  blocking collectives  52.8 us (7%)
  waiting for transfers between devices  44.8 us (6%)
  matrix products  30.4 us (4%)
  between operations  20.3 us (3%)
  starting transfers between devices  11.6 us (2%)
    sub x60, other arithmetic, batched_cholesky_solve(): work = work - column[:, None, :] * column[None, :, :]  325 us
    unnamed x417, local copies, waits for them, and re-layouts  46.4 us
    psum x1, blocking collectives, shards(): ccd_table = lax.psum(ccd_local, ('field', 'shard'))  44.1 us
    reduce_scatter x1, waiting for transfers between devices, shards(): summed = lax.psum_scatter(table, 'field', scatter_dimension=0, tiled=True)  39.1 us
    sub x58, other arithmetic, batched_cholesky_solve(): remain = remain - lower[:, step] * value[None, :]  35.9 us
    select_n x118, other arithmetic, batched_cholesky_solve(): column = jnp.where((rows_idx >= step)[:, None], column, jnp.float32(0.0))  35 us
    dot_general x6, matrix products, outer(): jnp.einsum('...ps,...qs->...pq', basis * scale[..., None, :], basis, prec...  17.7 us
  transfers between devices with their start and end apart: 3, of which 2 were waited for; matrix products, arithmetic and copies ran while one was open for 4% of the time, Pallas kernels for 0%

commit v1 on v0

v1 whole, which is shorter than its diff:
```python
import functools
import math

import jax
import jax.numpy as jnp
import numpy as np
from jax import lax
from jax.experimental import pallas as pl
from jax.experimental.pallas import tpu as pltpu
from jax.sharding import PartitionSpec as P

ORDER = 6
POLY = 28
NCCD = 189
LANES = 128
MESH = pl.DeviceIdType.MESH

STAR_DAMP = 0.1
EXPOSURE_DAMP = 1.0
DETECTOR_DAMP = 1.0

DEGREE = 2 * ORDER
BLOCK = 96
AT_GRAD = 3 * BLOCK
AT_ROW = AT_GRAD + 2 * POLY
AT_CCD = AT_ROW + 8
WIDTH = 384
AT_DET = 64
BF = jnp.bfloat16
F32 = jnp.float32

PAIRS = [(first, total - first) for total in range(ORDER + 1) for first in range(total + 1)]
MOMENTS = [(first, second) for first in range(DEGREE + 1) for second in range(DEGREE + 1 - first)]
SPOT = {pair: at for at, pair in enumerate(MOMENTS)}
CCD_MOMENTS = [(0, 0), (1, 0), (0, 1), (2, 0), (1, 1), (0, 2)]
SIZE = 2 * POLY
TILES = SIZE // 8


def base_of(row):
    return sum(TILES - r // 8 for r in range(row))


def tile_at(row, column_tile):
    return 8 * (base_of(row) + column_tile - row // 8)


def bf16_parts(values):
    parts = []
    rest = np.asarray(values, np.float32)
    for _ in range(3):
        high = rest.astype(BF)
        parts.append(high)
        rest = (rest - high.astype(np.float32)).astype(np.float32)
    return np.stack(parts)


@functools.lru_cache(maxsize=None)
def expansion():
    lin = np.zeros((ORDER + 1, ORDER + 1, DEGREE + 1))
    for i in range(ORDER + 1):
        for j in range(ORDER + 1):
            one, two = np.zeros(i + 1), np.zeros(j + 1)
            one[i], two[j] = 1.0, 1.0
            prod = np.polynomial.legendre.legmul(one, two)
            lin[i, j, : len(prod)] = prod
    pair = np.zeros((POLY, POLY, BLOCK))
    for p, (i, j) in enumerate(PAIRS):
        for q, (k, l) in enumerate(PAIRS):
            scale = math.sqrt((2 * i + 1) * (2 * j + 1) * (2 * k + 1) * (2 * l + 1))
            for at, (a, b) in enumerate(MOMENTS):
                pair[p, q, at] = scale * lin[i, k, a] * lin[j, l, b]
    top, low = [], []
    for row in range(SIZE):
        for col in range(8 * (row // 8), SIZE):
            line = np.zeros(3 * BLOCK)
            kind = row // POLY + col // POLY
            line[kind * BLOCK : (kind + 1) * BLOCK] = pair[row % POLY, col % POLY]
            if row == col:
                line[kind * BLOCK + len(MOMENTS)] = EXPOSURE_DAMP
            if row < POLY:
                top.append(line[: 2 * BLOCK])
            else:
                low.append(line[2 * BLOCK :])
    return bf16_parts(np.stack(top)), bf16_parts(np.stack(low))


def split3(x):
    high = x.astype(BF)
    rest = x - high.astype(F32)
    mid = rest.astype(BF)
    low = (rest - mid.astype(F32)).astype(BF)
    return high, mid, low


def dot(a, b):
    return jnp.dot(a, b, preferred_element_type=F32)


def dot_nt(a, b):
    return lax.dot_general(a, b, (((1,), (1,)), ((), ())), preferred_element_type=F32)


def series(value, degree_max):
    values = [jnp.ones_like(value), value]
    for degree in range(1, degree_max):
        values.append(
            (2 * degree + 1) / (degree + 1) * value * values[degree]
            - degree / (degree + 1) * values[degree - 1]
        )
    return values


def iota(shape, axis):
    return lax.broadcasted_iota(jnp.int32, shape, axis)


def star_parts(tiles, visits, off_ref, wd_ref, wc_ref, cnt_ref):
    square = iota((tiles, tiles), 0) == iota((tiles, tiles), 1)
    count = jnp.sum(jnp.where(square, cnt_ref[...].astype(F32), 0.0), axis=1, keepdims=True)
    present = (iota((tiles, LANES), 1).astype(F32) < count).astype(F32)
    weights, resid = [], []
    for k in range(visits):
        d0 = wd_ref[pl.ds(2 * k, tiles, stride=2 * visits), :]
        d1 = wd_ref[pl.ds(2 * k + 1, tiles, stride=2 * visits), :]
        corr = wc_ref[k * tiles : (k + 1) * tiles, :]
        weights.append((d0 * present, d1 * present, corr * jnp.sqrt(d0 * d1) * present))
        resid.append(
            (
                off_ref[pl.ds(2 * k, tiles, stride=2 * visits), :],
                off_ref[pl.ds(2 * k + 1, tiles, stride=2 * visits), :],
            )
        )
    hess_xx = sum(w[0] for w in weights) + STAR_DAMP
    hess_yy = sum(w[1] for w in weights) + STAR_DAMP
    hess_xy = sum(w[2] for w in weights)
    inv_det = 1.0 / (hess_xx * hess_yy - hess_xy * hess_xy)
    return weights, resid, (hess_yy * inv_det, hess_xx * inv_det, -hess_xy * inv_det)


def gradient(weights, resid):
    grad_x = sum(w[0] * r[0] + w[2] * r[1] for w, r in zip(weights, resid))
    grad_y = sum(w[2] * r[0] + w[1] * r[1] for w, r in zip(weights, resid))
    return grad_x, grad_y


def visit_row(ids, tiles, visits):
    spread = (iota((tiles, LANES), 1) % tiles == iota((tiles, LANES), 0)).astype(F32)
    rows = jnp.dot(
        ids.astype(F32), spread, precision=lax.Precision.HIGHEST, preferred_element_type=F32
    )
    keep = iota((visits, LANES), 0) == iota((visits, LANES), 1) // tiles
    return jnp.sum(jnp.where(keep, rows, 0.0), axis=0, keepdims=True)


def moments_kernel(
    tiles, visits, devices, cap, exp_local,
    uv_ref, off_ref, wd_ref, wc_ref, cnt_ref, eid_ref, cid_ref, slot_ref,
    out_ref, tgt_ref, leg_v, part,
):
    count = tiles * visits
    weights, resid, (inv_xx, inv_yy, inv_xy) = star_parts(
        tiles, visits, off_ref, wd_ref, wc_ref, cnt_ref
    )
    grad_x, grad_y = gradient(weights, resid)
    shift_x = inv_xx * grad_x + inv_xy * grad_y
    shift_y = inv_xy * grad_x + inv_yy * grad_y
    lists = [[] for _ in range(7)]
    for k in range(visits):
        wxx, wyy, wxy = weights[k]
        left_x, left_y = resid[k][0] - shift_x, resid[k][1] - shift_y
        prod_11 = inv_xx * wxx + inv_xy * wxy
        prod_12 = inv_xx * wxy + inv_xy * wyy
        prod_21 = inv_xy * wxx + inv_yy * wxy
        prod_22 = inv_xy * wxy + inv_yy * wyy
        for at, value in enumerate(
            (
                uv_ref[pl.ds(2 * k, tiles, stride=2 * visits), :],
                uv_ref[pl.ds(2 * k + 1, tiles, stride=2 * visits), :],
                wxx - (wxx * prod_11 + wxy * prod_21),
                wxy - (wxx * prod_12 + wxy * prod_22),
                wyy - (wxy * prod_12 + wyy * prod_22),
                wxx * left_x + wxy * left_y,
                wxy * left_x + wyy * left_y,
            )
        ):
            lists[at].append(value)
    pad = jnp.zeros((LANES - count, LANES), F32)
    cols = [jnp.concatenate(group + [pad], axis=0).T for group in lists]
    u, v = cols[0], cols[1]
    leg_u = series(u, DEGREE)
    for b, value in enumerate(series(v, DEGREE)):
        leg_v[b] = value

    def fold(value):
        return jnp.sum(value.reshape(LANES // 8, 8, LANES), axis=0)

    def put(row, value):
        part[8 * row : 8 * row + 8, :] = value

    zero = jnp.zeros((8, LANES), F32)
    for row in range(WIDTH):
        if row < AT_GRAD and row % BLOCK >= len(MOMENTS) or row >= AT_ROW:
            put(row, zero)
    for kind in range(3):
        weight = cols[2 + kind]
        for a in range(DEGREE + 1):
            scaled = weight * leg_u[a] if a else weight
            for b in range(DEGREE + 1 - a):
                value = scaled * leg_v[b] if b else scaled
                put(kind * BLOCK + SPOT[a, b], fold(value))
    for axis in range(2):
        pull = cols[5 + axis]
        for a in range(ORDER + 1):
            scaled = pull * leg_u[a] if a else pull
            for b in range(ORDER + 1 - a):
                value = scaled * leg_v[b] if b else scaled
                norm = math.sqrt((2 * a + 1) * (2 * b + 1))
                put(AT_GRAD + axis * POLY + PAIRS.index((a, b)), fold(value) * norm)
    vec = part[pl.ds(0, WIDTH, stride=8), :]
    for s in range(1, 8):
        vec = vec + part[pl.ds(s, WIDTH, stride=8), :]

    exp_id = visit_row(eid_ref[...], tiles, visits).astype(jnp.int32)
    ccd_id = visit_row(cid_ref[...], tiles, visits).astype(jnp.int32)
    groups = slot_ref.shape[0]
    pick = (iota((groups, LANES), 0) == exp_id // LANES).astype(F32)
    looked = lax.dot_general(
        slot_ref[...].astype(F32), pick, (((0,), (0,)), ((), ())),
        precision=lax.Precision.HIGHEST, preferred_element_type=F32,
    )
    inside = iota((LANES, LANES), 0) == exp_id % LANES
    place = jnp.sum(jnp.where(inside, looked, 0.0), axis=0, keepdims=True).astype(jnp.int32)
    valid = iota((1, LANES), 1) < count
    dest = jnp.where(valid, place // exp_local, -1)
    local_row = place % exp_local
    marks = (iota((devices, LANES), 0) == dest).astype(F32)
    before = (iota((LANES, LANES), 0) < iota((LANES, LANES), 1)).astype(BF)
    rank = jnp.sum(marks * dot(marks.astype(BF), before), axis=0, keepdims=True)
    target = jnp.where(valid, dest * cap + rank.astype(jnp.int32), -1)
    ccd_id = jnp.where(valid, ccd_id, -1)
    slots = devices * cap
    send = (iota((slots, LANES), 0) == target).astype(F32).astype(BF)
    seen = (iota((slots, LANES), 0) == ccd_id).astype(F32).astype(BF)
    tgt_ref[...] = jnp.where(iota((8, LANES), 0) == 0, target, ccd_id)

    vec = jnp.where(iota((WIDTH, LANES), 0) == AT_ROW, (local_row + 1).astype(F32), vec)
    out = sum(dot_nt(send, piece) for piece in split3(vec))
    picked = [vec[kind * BLOCK + SPOT[m] : kind * BLOCK + SPOT[m] + 1] for kind in range(3) for m in CCD_MOMENTS]
    for axis in range(2):
        for m in ((0, 0), (1, 0), (0, 1)):
            at = AT_GRAD + axis * POLY + PAIRS.index(m)
            picked.append(vec[at : at + 1])
    shift = AT_CCD - 2 * LANES
    ccd_vec = jnp.concatenate(
        [jnp.zeros((shift, LANES), F32)] + picked
        + [jnp.zeros((LANES - shift - len(picked), LANES), F32)], axis=0,
    )
    tail = out[:, 2 * LANES :] + sum(dot_nt(seen, piece) for piece in split3(ccd_vec))
    out_ref[...] = jnp.concatenate([out[:, : 2 * LANES], tail], axis=1)


def exchange_kernel(fields, shards_n, src_ref, dst_ref, send_sem, recv_sem, own_sem):
    devices = fields * shards_n
    me = lax.axis_index("field") * shards_n + lax.axis_index("shard")
    barrier = pltpu.get_barrier_semaphore()

    def greet(step, carry):
        peer = lax.rem(me + step, devices)
        pl.semaphore_signal(
            barrier, inc=1, device_id=(peer // shards_n, peer % shards_n), device_id_type=MESH
        )
        return carry

    lax.fori_loop(1, devices, greet, 0)
    own = pltpu.make_async_copy(src_ref.at[me], dst_ref.at[me], own_sem)
    own.start()
    pl.semaphore_wait(barrier, devices - 1)

    def copy(step):
        peer = lax.rem(me + step, devices)
        return pltpu.make_async_remote_copy(
            src_ref=src_ref.at[peer],
            dst_ref=dst_ref.at[me],
            send_sem=send_sem.at[step],
            recv_sem=recv_sem.at[step],
            device_id=(peer // shards_n, peer % shards_n),
            device_id_type=MESH,
        )

    def launch(step, carry):
        copy(step).start()
        return carry

    def finish(step, carry):
        copy(step).wait_send()
        origin = lax.rem(me - step + devices, devices)
        pltpu.make_async_remote_copy(
            src_ref=src_ref.at[me],
            dst_ref=dst_ref.at[origin],
            send_sem=send_sem.at[step],
            recv_sem=recv_sem.at[step],
            device_id=(origin // shards_n, origin % shards_n),
            device_id_type=MESH,
        ).wait_recv()
        return carry

    lax.fori_loop(1, devices, launch, 0)
    own.wait()
    lax.fori_loop(1, devices, finish, 0)


def exchange(values, fields, shards_n, collective_id):
    devices = fields * shards_n
    return pl.pallas_call(
        functools.partial(exchange_kernel, fields, shards_n),
        out_shape=jax.ShapeDtypeStruct(values.shape, values.dtype),
        in_specs=[pl.BlockSpec(memory_space=pltpu.VMEM)],
        out_specs=pl.BlockSpec(memory_space=pltpu.VMEM),
        scratch_shapes=[
            pltpu.SemaphoreType.DMA((devices,)),
            pltpu.SemaphoreType.DMA((devices,)),
            pltpu.SemaphoreType.DMA,
        ],
        compiler_params=pltpu.CompilerParams(collective_id=collective_id, has_side_effects=True),
    )(values)


def small_solve(matrix, rhs):
    size = len(rhs)
    work = [list(line) for line in matrix]
    rhs = list(rhs)
    inverse = []
    for k in range(size):
        inv = 1.0 / work[k][k]
        inverse.append(inv)
        for r in range(k + 1, size):
            coef = work[k][r] * inv
            for c in range(r, size):
                work[r][c] = work[r][c] - coef * work[k][c]
            rhs[r] = rhs[r] - coef * rhs[k]
    out = [None] * size
    for k in range(size - 1, -1, -1):
        value = rhs[k]
        for c in range(k + 1, size):
            value = value - work[k][c] * out[c]
        out[k] = value * inverse[k]
    return out


def solve_kernel(cap, recv_ref, top_ref, low_ref, exp_ref, back_ref, mat, coefs, dinv):
    slots = recv_ref.shape[0]
    exp_local = exp_ref.shape[1]
    recv = recv_ref[...]
    flipped = recv.T
    rows = recv[:, AT_ROW : AT_ROW + 1]
    own = ((iota((slots, exp_local), 1) + 1).astype(F32) == rows).astype(F32).astype(BF)
    det = (iota((slots, exp_local), 1) == iota((slots, exp_local), 0) % cap).astype(F32).astype(BF)
    parts = split3(flipped)
    table = sum(dot(piece[:AT_CCD], own) for piece in parts)
    ccd = sum(dot(piece[AT_CCD:], det) for piece in parts)

    row_at = iota((AT_GRAD, exp_local), 0)
    damp = (row_at == len(MOMENTS)) | (row_at == 2 * BLOCK + len(MOMENTS))
    held = split3(jnp.where(damp, 1.0, table[:AT_GRAD]))
    split_at = top_ref.shape[1]
    for source, first, last, begin in ((top_ref, 0, 2 * BLOCK, 0), (low_ref, 2 * BLOCK, 3 * BLOCK, split_at)):
        total = None
        for i, j in ((0, 2), (1, 1), (2, 0), (0, 1), (1, 0), (0, 0)):
            term = dot(source[i], held[j][first:last])
            total = term if total is None else total + term
        mat[begin : begin + source.shape[1], :] = total

    sub = iota((8, exp_local), 0)
    grad = [table[AT_GRAD + 8 * t : AT_GRAD + 8 * t + 8] for t in range(TILES)]
    for kb in range(TILES):
        block = [
            [mat[tile_at(8 * kb + r, jt) : tile_at(8 * kb + r, jt) + 8, :] for jt in range(kb, TILES)]
            for r in range(8)
        ]
        for r in range(8):
            inv = 1.0 / block[r][0][r : r + 1]
            dinv[8 * kb + r : 8 * kb + r + 1, :] = inv
            scaled = [tile * inv for tile in block[r]]
            for at, tile in enumerate(scaled):
                coefs[r, 8 * (kb + at) : 8 * (kb + at) + 8, :] = tile
            for r2 in range(r + 1, 8):
                coef = scaled[0][r2 : r2 + 1]
                block[r2] = [x - coef * y for x, y in zip(block[r2], block[r])]
            step = grad[kb][r : r + 1]
            grad[kb] = grad[kb] - jnp.where(sub > r, scaled[0] * step, 0.0)
            for at in range(1, TILES - kb):
                grad[kb + at] = grad[kb + at] - scaled[at] * step
        for r in range(8):
            for at, tile in enumerate(block[r]):
                start = tile_at(8 * kb + r, kb + at)
                mat[start : start + 8, :] = tile
        for jt in range(kb + 1, TILES):
            for row in range(8 * kb + 8, 8 * jt + 8):
                start = tile_at(row, jt)
                value = mat[start : start + 8, :]
                for r in range(8):
                    value = value - coefs[r, row : row + 1, :] * block[r][jt - kb]
                mat[start : start + 8, :] = value

    answer = [None] * TILES
    for kb in range(TILES - 1, -1, -1):
        rest, inner = [], []
        for r in range(8):
            line = grad[kb][r : r + 1]
            if kb + 1 < TILES:
                total = None
                for jt in range(kb + 1, TILES):
                    start = tile_at(8 * kb + r, jt)
                    term = mat[start : start + 8, :] * answer[jt]
                    total = term if total is None else total + term
                line = line - jnp.sum(total, axis=0, keepdims=True)
            rest.append(line)
            start = tile_at(8 * kb + r, kb)
            inner.append(mat[start : start + 8, :])
        found = [None] * 8
        for r in range(7, -1, -1):
            found[r] = rest[r] * dinv[8 * kb + r : 8 * kb + r + 1, :]
            for r2 in range(r):
                rest[r2] = rest[r2] - inner[r2][r : r + 1] * found[r]
        answer[kb] = jnp.concatenate(found, axis=0)
    solved = jnp.concatenate(answer, axis=0)
    exp_ref[...] = solved

    lines = [ccd[i : i + 1] for i in range(24)]
    grams = []
    for kind in range(3):
        m00, m10, m01, m20, m11, m02 = lines[6 * kind : 6 * kind + 6]
        uu = (2.0 * m20 + m00) * (1.0 / 3.0)
        vv = (2.0 * m02 + m00) * (1.0 / 3.0)
        grams.append([[m00, m10, m01], [m10, uu, m11], [m01, m11, vv]])
    root = 1.0 / math.sqrt(3.0)
    rhs = [lines[18], lines[19] * root, lines[20] * root, lines[21], lines[22] * root, lines[23] * root]
    matrix = [
        [grams[i // 3 + j // 3][i % 3][j % 3] + (DETECTOR_DAMP if i == j else 0.0) for j in range(6)]
        for i in range(6)
    ]
    det_update = small_solve(matrix, rhs)

    exp_rows = jnp.concatenate([solved, jnp.zeros((LANES - SIZE, exp_local), F32)], axis=0)
    det_rows = jnp.concatenate(
        [jnp.zeros((AT_DET, exp_local), F32)] + det_update
        + [jnp.zeros((LANES - AT_DET - 6, exp_local), F32)], axis=0,
    )
    back = sum(dot_nt(own, piece) for piece in split3(exp_rows))
    back_ref[...] = back + sum(dot_nt(det, piece) for piece in split3(det_rows))


def stars_kernel(
    tiles, visits, uv_ref, off_ref, wd_ref, wc_ref, cnt_ref, tgt_ref, back_ref, star_ref, ccd_ref
):
    back = back_ref[...]
    slots = back.shape[0]
    ccd_ref[...] = back[:NCCD, AT_DET : AT_DET + 6]
    pieces = split3(back)

    def take(row):
        wide = jnp.broadcast_to(tgt_ref[row : row + 1, :].astype(F32), (LANES, LANES)).T
        wide = jnp.concatenate([wide] * (slots // LANES), axis=1)
        chosen = (iota((LANES, slots), 1).astype(F32) == wide).astype(F32).astype(BF)
        return sum(dot(chosen, piece) for piece in pieces)

    exp_coef = take(0)
    det_coef = take(1)
    weights, resid, (inv_xx, inv_yy, inv_xy) = star_parts(
        tiles, visits, off_ref, wd_ref, wc_ref, cnt_ref
    )
    root = 1.0 / math.sqrt(3.0)
    moved = []
    for k in range(visits):
        u = uv_ref[pl.ds(2 * k, tiles, stride=2 * visits), :]
        v = uv_ref[pl.ds(2 * k + 1, tiles, stride=2 * visits), :]
        leg_u = [x * math.sqrt(2 * n + 1) for n, x in enumerate(series(u, ORDER))]
        leg_v = [x * math.sqrt(2 * n + 1) for n, x in enumerate(series(v, ORDER))]
        lines = slice(k * tiles, (k + 1) * tiles)
        model = []
        for axis in range(2):
            extra = {(0, 0): (0, 1.0), (1, 0): (1, root), (0, 1): (2, root)}
            total = None
            for a in range(ORDER + 1):
                inner = None
                for b in range(ORDER + 1 - a):
                    at = axis * POLY + PAIRS.index((a, b))
                    coef = exp_coef[lines, at : at + 1]
                    if (a, b) in extra:
                        where, scale = extra[a, b]
                        where += AT_DET + 3 * axis
                        coef = coef + det_coef[lines, where : where + 1] * scale
                    term = coef * leg_v[b] if b else jnp.broadcast_to(coef, u.shape)
                    inner = term if inner is None else inner + term
                term = leg_u[a] * inner if a else inner
                total = term if total is None else total + term
            model.append(total)
        moved.append((resid[k][0] - model[0], resid[k][1] - model[1]))
    grad_x, grad_y = gradient(weights, moved)
    star_ref[pl.ds(0, tiles, stride=2), :] = inv_xx * grad_x + inv_xy * grad_y
    star_ref[pl.ds(1, tiles, stride=2), :] = inv_xy * grad_x + inv_yy * grad_y


def plain(kernel, out_shape, scratch=()):
    return pl.pallas_call(
        kernel,
        out_shape=out_shape,
        scratch_shapes=list(scratch),
        compiler_params=pltpu.CompilerParams(vmem_limit_bytes=48 * 1024 * 1024),
    )


def shards(focal_uv, offsets, w_diag, w_corr, star_count, exposure_ids, ccd_ids, exp_slot):
    shards_n = lax.axis_size("shard")
    fields = lax.axis_size("field")
    devices = shards_n * fields
    tiles, visits, _, stars = offsets.shape
    cap = 2 * tiles * visits // (3 * shards_n)
    slots = devices * cap
    exp_local = exp_slot.shape[0] // devices
    assert slots >= NCCD and slots % LANES == 0 and tiles * visits <= LANES and stars == LANES
    sds = jax.ShapeDtypeStruct
    uv = focal_uv.reshape(tiles * visits * 2, stars)
    off = offsets.reshape(tiles * visits * 2, stars)
    wd = w_diag.reshape(tiles * visits * 2, stars)
    wc = w_corr.transpose(1, 0, 2).reshape(tiles * visits, stars)
    cnt = star_count.reshape(1, tiles)
    out, tgt = plain(
        functools.partial(moments_kernel, tiles, visits, devices, cap, exp_local),
        (sds((slots, WIDTH), F32), sds((8, LANES), jnp.int32)),
        (pltpu.VMEM((DEGREE + 1, stars, LANES), F32), pltpu.VMEM((8 * WIDTH, LANES), F32)),
    )(uv, off, wd, wc, cnt, exposure_ids.T, ccd_ids.T, exp_slot.reshape(-1, LANES))
    recv = exchange(out.reshape(devices, cap, WIDTH), fields, shards_n, 0).reshape(slots, WIDTH)
    top, low = expansion()
    exposure_update, back = plain(
        functools.partial(solve_kernel, cap),
        (sds((SIZE, exp_local), F32), sds((slots, LANES), F32)),
        (
            pltpu.VMEM((8 * base_of(SIZE), exp_local), F32),
            pltpu.VMEM((8, SIZE, exp_local), F32),
            pltpu.VMEM((SIZE, exp_local), F32),
        ),
    )(recv, jnp.asarray(top), jnp.asarray(low))
    got = exchange(back.reshape(devices, cap, LANES), fields, shards_n, 1).reshape(slots, LANES)
    star_update, ccd_update = plain(
        functools.partial(stars_kernel, tiles, visits),
        (sds((tiles * 2, stars), F32), sds((NCCD, 6), F32)),
    )(uv, off, wd, wc, cnt, tgt, got)
    return star_update.reshape(tiles, 2, stars), exposure_update, ccd_update


def solution(mesh):
    in_specs = (
        P(("field", "shard"), None, None, None),
        P(("field", "shard"), None, None, None),
        P(("field", "shard"), None, None, None),
        P(("field", "shard"), None, None),
        P(("field", "shard")),
        P(("field", "shard"), None),
        P(("field", "shard"), None),
        P(),
    )
    out_specs = (P(("field", "shard"), None, None), P(None, ("field", "shard")), P())
    return jax.shard_map(shards, mesh=mesh, in_specs=in_specs, out_specs=out_specs, check_vma=False)
```

time: 733 us -> 54.8 us (0.07); the launches traced: 718 us -> 54.3 us
  other arithmetic: 450 us -> 0 us
  local copies, waits for them, and re-layouts: 108 us -> 12.7 us
  blocking collectives: 52.8 us -> 0 us
  waiting for transfers between devices: 44.8 us -> 0 us
  Pallas kernels: 0 us -> 40.8 us
  matrix products: 30.4 us -> 0 us
  between operations: 20.3 us -> 0.75 us
  starting transfers between devices: 11.6 us -> 0 us
    sub x176 -> x0, other arithmetic: 375 us -> none  [the longest x60 325 us: batched_cholesky_solve(): work = work - column[:, None, :] * column[None, :, :]]
    psum x1 -> x0, blocking collectives: 44.1 us -> none  [shards(): ccd_table = lax.psum(ccd_local, ('field', 'shard'))]
    pallas_call x0 -> x5, Pallas kernels: none -> 40.8 us  [the longest x2 29.7 us: exchange(): pl.pallas_call(functools.partial(exchange_kernel, fields, shards_n), out_...]
    reduce_scatter x1 -> x0, waiting for transfers between devices: 39.1 us -> none  [shards(): summed = lax.psum_scatter(table, 'field', scatter_dimension=0, tiled=True)]
    select_n x122 -> x0, other arithmetic: 35.9 us -> none  [the longest x118 35 us: batched_cholesky_solve(): column = jnp.where((rows_idx >= step)[:, None], column, jnp.float32(0.0))]
    unnamed x417 -> x39, local copies, waits for them, and re-layouts: 46.4 us -> 12.7 us
    dot_general x14 -> x0, matrix products: 30.4 us -> none  [the longest x6 17.7 us: outer(): jnp.einsum('...ps,...qs->...pq', basis * scale[..., None, :], basis, prec...]
    another operation x7 -> x0, local copies, waits for them, and re-layouts: 21.6 us -> none  [the longest x2 12.2 us: batched_cholesky_solve(): lower = jnp.stack(columns, axis=1)]
  transfers between devices with their start and end apart: 3 -> 0, of which waited for: 2 -> 0; matrix products, arithmetic and copies ran while one was open for 4% -> 0% of each run, Pallas kernels for 0% -> 0%
where the time goes in v1:
time: 54.8 us; the launch traced here: 54.3 us
  Pallas kernels  40.8 us (74%)
  local copies, waits for them, and re-layouts  12.7 us (23%)
  between operations  0.75 us (1%)
    pallas_call x2, Pallas kernels, exchange(): pl.pallas_call(functools.partial(exchange_kernel, fields, shards_n), out_...  29.7 us
    unnamed x39, local copies, waits for them, and re-layouts  12.7 us
    pallas_call x1, Pallas kernels, shards(): plain(functools.partial(solve_kernel, cap), (sds((SIZE, exp_local), F32),...  4.38 us
    pallas_call x1, Pallas kernels, shards(): plain(functools.partial(stars_kernel, tiles, visits), (sds((tiles * 2, st...  4.15 us
    pallas_call x1, Pallas kernels, shards(): plain(functools.partial(moments_kernel, tiles, visits, devices, cap, exp_...  2.52 us

profile of v1, /device:TPU:0, one launch (start us, length us, event | category | flops | bytes accessed | tf_op | source)
XLA Modules:
  0.0 54.3 jit_solution(14451361732731961089)
XLA Ops:
  0.6 0.0 copy-start.4
  0.6 0.9 %copy-done.4 = f32[16,6,2,128]{3,2,1,0:T(2,128)S(1)} copy-done((f32[16,6,2,128]{3,2,1,0:T(2,128)S(1)}, f32[16,6,2,128]{3,2,1,0:T(2,128)}, u32[]{:S(2)}) %copy-start.4) | copy-done | bytes 98328
  1.5 0.0 copy-start.6
  1.5 0.9 %copy-done.6 = f32[16,6,2,128]{3,2,1,0:T(2,128)S(1)} copy-done((f32[16,6,2,128]{3,2,1,0:T(2,128)S(1)}, f32[16,6,2,128]{3,2,1,0:T(2,128)}, u32[]{:S(2)}) %copy-start.6) | copy-done | bytes 98328
  2.4 0.0 copy-start.8
  2.4 0.9 %copy-done.8 = f32[16,6,2,128]{3,2,1,0:T(2,128)S(1)} copy-done((f32[16,6,2,128]{3,2,1,0:T(2,128)S(1)}, f32[16,6,2,128]{3,2,1,0:T(2,128)}, u32[]{:S(2)}) %copy-start.8) | copy-done | bytes 98328
  3.3 0.8 %copy-done.11 = f32[16,6,128]{2,0,1:T(8,128)S(1)} copy-done((f32[16,6,128]{2,0,1:T(8,128)S(1)}, f32[16,6,128]{2,0,1:T(8,128)}, u32[]{:S(2)}) %copy-start.11) | copy-done | bytes 49176
  4.1 0.7 %copy-done.14 = s32[4096]{0:T(1024)S(1)} copy-done((s32[4096]{0:T(1024)S(1)}, s32[4096]{0:T(1024)}, u32[]{:S(2)}) %copy-start.14) | copy-done | bytes 16408
  4.8 0.7 %copy-done.15 = s32[16,6]{0,1:T(8,128)S(1)} copy-done((s32[16,6]{0,1:T(8,128)S(1)}, s32[16,6]{0,1:T(8,128)}, u32[]{:S(2)}) %copy-start.15) | copy-done | bytes 408
  5.5 0.7 %copy-done.16 = s32[16,6]{0,1:T(8,128)S(1)} copy-done((s32[16,6]{0,1:T(8,128)S(1)}, s32[16,6]{0,1:T(8,128)}, u32[]{:S(2)}) %copy-start.16) | copy-done | bytes 408
  6.2 0.7 %copy-done.17 = s32[16]{0:T(128)S(1)} copy-done((s32[16]{0:T(128)S(1)}, s32[16]{0:T(128)}, u32[]{:S(2)}) %copy-start.17) | copy-done | bytes 88
  6.9 2.5 %shard_map.121 = (f32[256,384]{1,0:T(8,128)S(1)}, s32[8,128]{1,0:T(8,128)S(1)}) custom-call(f32[192,128]{1,0:T(8,128)S(1)} %bitcast.18, f32[192,128]{1,0:T(8,128)S(1)} %bitcast.20, f32[192,128]{1,0:T(8,128)S(1)} %bitcast.22, f32[96,128]{1,0:T(8,128)S(1)} %bitcast.24, s32[1,16]{1,0:T(1,128)S(1)} %bitcast.30, s32[6,16]{1,0:T(8,128)S(1)} %bitcast.28, ...), custom_call_target="tpu_custom_call" | custom-call | tf_op jit(solution)/shard_map/pallas_call | solution.py:529
  9.4 0.0 copy-start.3
  9.4 0.7 %copy-done.3 = f32[256,384]{1,0:T(8,128)} copy-done((f32[256,384]{1,0:T(8,128)}, f32[256,384]{1,0:T(8,128)S(1)}, u32[]{:S(2)}) %copy-start.3) | copy-done | bytes 393240
  10.2 0.0 copy-start.18
  10.2 18.6 %shard_map.122 = f32[32,8,384]{2,1,0:T(8,128)} custom-call(f32[32,8,384]{2,1,0:T(8,128)} %bitcast.17), custom_call_target="tpu_custom_call" | custom-call | tf_op jit(solution)/shard_map/pallas_call | solution.py:315
  28.8 0.0 copy-start
  28.8 1.5 %copy-done = bf16[3,1280,192]{2,1,0:T(8,128)(2,1)S(1)} copy-done((bf16[3,1280,192]{2,1,0:T(8,128)(2,1)S(1)}, bf16[3,1280,192]{2,1,0:T(8,128)(2,1)}, u32[]{:S(2)}) %copy-start) | copy-done | bytes 1474584
  30.3 1.0 %copy-done.1 = f32[32,8,384]{2,1,0:T(8,128)S(1)} copy-done((f32[32,8,384]{2,1,0:T(8,128)S(1)}, f32[32,8,384]{2,1,0:T(8,128)}, u32[]{:S(2)}) %copy-start.1) | copy-done | bytes 393240
  31.3 1.0 %copy-done.10 = bf16[3,512,96]{2,1,0:T(8,128)(2,1)S(1)} copy-done((bf16[3,512,96]{2,1,0:T(8,128)(2,1)S(1)}, bf16[3,512,96]{2,1,0:T(8,128)(2,1)}, u32[]{:S(2)}) %copy-start.10) | copy-done | bytes 294936
  32.3 4.4 %shard_map.123 = (f32[56,128]{1,0:T(8,128)}, f32[256,128]{1,0:T(8,128)S(1)}) custom-call(f32[256,384]{1,0:T(8,128)S(1)} %bitcast.15, bf16[3,1280,192]{2,1,0:T(8,128)(2,1)S(1)} %copy-done, bf16[3,512,96]{2,1,0:T(8,128)(2,1)S(1)} %copy-done.10), custom_call_target="tpu_custom_call" | custom-call | tf_op jit(solution)/shard_map/pallas_call | solution.py:536
  36.7 0.6 %copy-done.13 = f32[256,128]{1,0:T(8,128)} copy-done((f32[256,128]{1,0:T(8,128)}, f32[256,128]{1,0:T(8,128)S(1)}, u32[]{:S(2)}) %copy-start.13) | copy-done | bytes 131096
  37.3 11.2 %shard_map.124 = f32[32,8,128]{2,1,0:T(8,128)} custom-call(f32[32,8,128]{2,1,0:T(8,128)} %bitcast.26), custom_call_target="tpu_custom_call" | custom-call | tf_op jit(solution)/shard_map/pallas_call | solution.py:315
  48.5 0.0 copy-done.5
  48.5 0.0 copy-done.7
  48.5 0.0 copy-done.9
  48.5 0.0 copy-done.12
  48.5 0.0 copy-done.18
  48.5 0.0 copy-start.2
  48.5 0.9 %copy-done.2 = f32[32,8,128]{2,1,0:T(8,128)S(1)} copy-done((f32[32,8,128]{2,1,0:T(8,128)S(1)}, f32[32,8,128]{2,1,0:T(8,128)}, u32[]{:S(2)}) %copy-start.2) | copy-done | bytes 131096
  49.4 4.1 %shard_map.125 = (f32[32,128]{1,0:T(8,128)}, f32[189,6]{1,0:T(8,128)S(1)}) custom-call(f32[192,128]{1,0:T(8,128)S(1)} %bitcast.19, f32[192,128]{1,0:T(8,128)S(1)} %bitcast.21, f32[192,128]{1,0:T(8,128)S(1)} %bitcast.23, f32[96,128]{1,0:T(8,128)S(1)} %bitcast.25, s32[1,16]{1,0:T(1,128)S(1)} %bitcast.31, s32[8,128]{1,0:T(8,128)S(1)} %get-tuple-element.9.tgt_ref, ...), custom_call_target="tpu_custom_call" | custom-call | tf_op jit(solution)/shard_map/pallas_call | solution.py:546
  53.6 0.7 %copy.13 = f32[189,6]{0,1:T(8,128)} copy(f32[189,6]{1,0:T(8,128)S(1)} %get-tuple-element.17) | data formatting | bytes 9072
  (12 shorter events, 0.0 us)
Async XLA Ops:
  0.6 0.9 %copy-start.4 = (f32[16,6,2,128]{3,2,1,0:T(2,128)S(1)}, f32[16,6,2,128]{3,2,1,0:T(2,128)}, u32[]{:S(2)}) copy-start(f32[16,6,2,128]{3,2,1,0:T(2,128)} %param.10) | copy-start | bytes 294916
  1.5 0.9 %copy-start.6 = (f32[16,6,2,128]{3,2,1,0:T(2,128)S(1)}, f32[16,6,2,128]{3,2,1,0:T(2,128)}, u32[]{:S(2)}) copy-start(f32[16,6,2,128]{3,2,1,0:T(2,128)} %param.11) | copy-start | bytes 294916
  2.4 0.9 %copy-start.8 = (f32[16,6,2,128]{3,2,1,0:T(2,128)S(1)}, f32[16,6,2,128]{3,2,1,0:T(2,128)}, u32[]{:S(2)}) copy-start(f32[16,6,2,128]{3,2,1,0:T(2,128)} %param.12) | copy-start | bytes 294916
  3.3 0.8 %copy-start.11 = (f32[16,6,128]{2,0,1:T(8,128)S(1)}, f32[16,6,128]{2,0,1:T(8,128)}, u32[]{:S(2)}) copy-start(f32[16,6,128]{2,0,1:T(8,128)} %param.13) | copy-start | bytes 147460
  4.1 0.7 %copy-start.14 = (s32[4096]{0:T(1024)S(1)}, s32[4096]{0:T(1024)}, u32[]{:S(2)}) copy-start(s32[4096]{0:T(1024)} %param.17) | copy-start | bytes 49156
  4.8 0.7 %copy-start.15 = (s32[16,6]{0,1:T(8,128)S(1)}, s32[16,6]{0,1:T(8,128)}, u32[]{:S(2)}) copy-start(s32[16,6]{0,1:T(8,128)} %param.15) | copy-start | bytes 1156
  5.5 0.7 %copy-start.16 = (s32[16,6]{0,1:T(8,128)S(1)}, s32[16,6]{0,1:T(8,128)}, u32[]{:S(2)}) copy-start(s32[16,6]{0,1:T(8,128)} %param.16) | copy-start | bytes 1156
  6.2 0.7 %copy-start.17 = (s32[16]{0:T(128)S(1)}, s32[16]{0:T(128)}, u32[]{:S(2)}) copy-start(s32[16]{0:T(128)} %param.14) | copy-start | bytes 196
  9.4 0.8 %copy-start.3 = (f32[256,384]{1,0:T(8,128)}, f32[256,384]{1,0:T(8,128)S(1)}, u32[]{:S(2)}) copy-start(f32[256,384]{1,0:T(8,128)S(1)} %get-tuple-element.10) | copy-start | bytes 1179652
  10.1 38.3 %copy-start.5 = (f32[16,6,2,128]{3,2,1,0:T(2,128)S(1)}, f32[16,6,2,128]{3,2,1,0:T(2,128)}, u32[]{:S(2)}) copy-start(f32[16,6,2,128]{3,2,1,0:T(2,128)} %param.10) | copy-start | bytes 294916
  10.1 38.3 %copy-start.7 = (f32[16,6,2,128]{3,2,1,0:T(2,128)S(1)}, f32[16,6,2,128]{3,2,1,0:T(2,128)}, u32[]{:S(2)}) copy-start(f32[16,6,2,128]{3,2,1,0:T(2,128)} %param.11) | copy-start | bytes 294916
  10.1 38.4 %copy-start.9 = (f32[16,6,2,128]{3,2,1,0:T(2,128)S(1)}, f32[16,6,2,128]{3,2,1,0:T(2,128)}, u32[]{:S(2)}) copy-start(f32[16,6,2,128]{3,2,1,0:T(2,128)} %param.12) | copy-start | bytes 294916
  10.1 38.4 %copy-start.12 = (f32[16,6,128]{2,0,1:T(8,128)S(1)}, f32[16,6,128]{2,0,1:T(8,128)}, u32[]{:S(2)}) copy-start(f32[16,6,128]{2,0,1:T(8,128)} %param.13) | copy-start | bytes 147460
  10.2 38.4 %copy-start.18 = (s32[16]{0:T(128)S(1)}, s32[16]{0:T(128)}, u32[]{:S(2)}) copy-start(s32[16]{0:T(128)} %param.14) | copy-start | bytes 196
  28.8 1.5 %copy-start = (bf16[3,1280,192]{2,1,0:T(8,128)(2,1)S(1)}, bf16[3,1280,192]{2,1,0:T(8,128)(2,1)}, u32[]{:S(2)}) copy-start(bf16[3,1280,192]{2,1,0:T(8,128)(2,1)} %constant.4.clone.top_ref) | copy-start | bytes 4423684
  30.3 1.0 %copy-start.1 = (f32[32,8,384]{2,1,0:T(8,128)S(1)}, f32[32,8,384]{2,1,0:T(8,128)}, u32[]{:S(2)}) copy-start(f32[32,8,384]{2,1,0:T(8,128)} %shard_map.122) | copy-start | bytes 1179652
  31.3 1.0 %copy-start.10 = (bf16[3,512,96]{2,1,0:T(8,128)(2,1)S(1)}, bf16[3,512,96]{2,1,0:T(8,128)(2,1)}, u32[]{:S(2)}) copy-start(bf16[3,512,96]{2,1,0:T(8,128)(2,1)} %constant.5.clone.low_ref) | copy-start | bytes 884740
  36.7 0.6 %copy-start.13 = (f32[256,128]{1,0:T(8,128)}, f32[256,128]{1,0:T(8,128)S(1)}, u32[]{:S(2)}) copy-start(f32[256,128]{1,0:T(8,128)S(1)} %get-tuple-element.11) | copy-start | bytes 393220
  48.5 0.9 %copy-start.2 = (f32[32,8,128]{2,1,0:T(8,128)S(1)}, f32[32,8,128]{2,1,0:T(8,128)}, u32[]{:S(2)}) copy-start(f32[32,8,128]{2,1,0:T(8,128)} %shard_map.124) | copy-start | bytes 393220

commit v2 on v1

--- a/solution.py
+++ b/solution.py
@@ -27,6 +27,7 @@
 WIDTH = 384
 AT_DET = 64
 BF = jnp.bfloat16
+HBM = pl.BlockSpec(memory_space=pltpu.HBM)
 F32 = jnp.float32
 
 PAIRS = [(first, total - first) for total in range(ORDER + 1) for first in range(total + 1)]
@@ -43,16 +44,6 @@
 
 def tile_at(row, column_tile):
     return 8 * (base_of(row) + column_tile - row // 8)
-
-
-def bf16_parts(values):
-    parts = []
-    rest = np.asarray(values, np.float32)
-    for _ in range(3):
-        high = rest.astype(BF)
-        parts.append(high)
-        rest = (rest - high.astype(np.float32)).astype(np.float32)
-    return np.stack(parts)
 
 
 @functools.lru_cache(maxsize=None)
@@ -82,7 +73,7 @@
                 top.append(line[: 2 * BLOCK])
             else:
                 low.append(line[2 * BLOCK :])
-    return bf16_parts(np.stack(top)), bf16_parts(np.stack(low))
+    return np.stack(top).astype(np.float32), np.stack(low).astype(np.float32)
 
 
 def split3(x):
@@ -155,10 +146,24 @@
 
 def moments_kernel(
     tiles, visits, devices, cap, exp_local,
-    uv_ref, off_ref, wd_ref, wc_ref, cnt_ref, eid_ref, cid_ref, slot_ref,
+    uv_any, off_any, wd_any, wc_any, cnt_any, eid_any, cid_any, slot_any,
     out_ref, tgt_ref, leg_v, part,
+    uv_ref, off_ref, wd_ref, wc_ref, cnt_ref, eid_ref, cid_ref, slot_ref, sems,
 ):
     count = tiles * visits
+    copies = [
+        pltpu.make_async_copy(source, target, sems.at[at])
+        for at, (source, target) in enumerate(
+            (
+                (wd_any, wd_ref), (off_any, off_ref), (wc_any, wc_ref), (cnt_any, cnt_ref),
+                (uv_any, uv_ref), (eid_any, eid_ref), (cid_any, cid_ref), (slot_any, slot_ref),
+            )
+        )
+    ]
+    for one in copies:
+        one.start()
+    for one in copies:
+        one.wait()
     weights, resid, (inv_xx, inv_yy, inv_xy) = star_parts(
         tiles, visits, off_ref, wd_ref, wc_ref, cnt_ref
     )
@@ -306,8 +311,8 @@
         return carry
 
     lax.fori_loop(1, devices, launch, 0)
+    lax.fori_loop(1, devices, finish, 0)
     own.wait()
-    lax.fori_loop(1, devices, finish, 0)
 
 
 def exchange(values, fields, shards_n, collective_id):
@@ -315,14 +320,16 @@
     return pl.pallas_call(
         functools.partial(exchange_kernel, fields, shards_n),
         out_shape=jax.ShapeDtypeStruct(values.shape, values.dtype),
-        in_specs=[pl.BlockSpec(memory_space=pltpu.VMEM)],
-        out_specs=pl.BlockSpec(memory_space=pltpu.VMEM),
+        in_specs=[pl.BlockSpec(memory_space=pltpu.HBM)],
+        out_specs=pl.BlockSpec(memory_space=pltpu.HBM),
         scratch_shapes=[
             pltpu.SemaphoreType.DMA((devices,)),
             pltpu.SemaphoreType.DMA((devices,)),
             pltpu.SemaphoreType.DMA,
         ],
-        compiler_params=pltpu.CompilerParams(collective_id=collective_id, has_side_effects=True),
+        compiler_params=pltpu.CompilerParams(
+            collective_id=collective_id, has_side_effects=True, vmem_limit_bytes=64 * 1024 * 1024
+        ),
     )(values)
 
 
@@ -348,7 +355,19 @@
     return out
 
 
-def solve_kernel(cap, recv_ref, top_ref, low_ref, exp_ref, back_ref, mat, coefs, dinv):
+def solve_kernel(
+    cap, recv_any, top_any, low_any, exp_ref, back_ref,
+    mat, coefs, dinv, recv_ref, top_ref, low_ref, sems,
+):
+    copies = [
+        pltpu.make_async_copy(source, target, sems.at[at])
+        for at, (source, target) in enumerate(
+            ((recv_any, recv_ref), (top_any, top_ref), (low_any, low_ref))
+        )
+    ]
+    for one in copies:
+        one.start()
+    copies[0].wait()
     slots = recv_ref.shape[0]
     exp_local = exp_ref.shape[1]
     recv = recv_ref[...]
@@ -363,13 +382,16 @@
     row_at = iota((AT_GRAD, exp_local), 0)
     damp = (row_at == len(MOMENTS)) | (row_at == 2 * BLOCK + len(MOMENTS))
     held = split3(jnp.where(damp, 1.0, table[:AT_GRAD]))
-    split_at = top_ref.shape[1]
+    split_at = top_ref.shape[0]
+    copies[1].wait()
+    copies[2].wait()
     for source, first, last, begin in ((top_ref, 0, 2 * BLOCK, 0), (low_ref, 2 * BLOCK, 3 * BLOCK, split_at)):
         total = None
+        pieces = split3(source[...])
         for i, j in ((0, 2), (1, 1), (2, 0), (0, 1), (1, 0), (0, 0)):
-            term = dot(source[i], held[j][first:last])
+            term = dot(pieces[i], held[j][first:last])
             total = term if total is None else total + term
-        mat[begin : begin + source.shape[1], :] = total
+        mat[begin : begin + source.shape[0], :] = total
 
     sub = iota((8, exp_local), 0)
     grad = [table[AT_GRAD + 8 * t : AT_GRAD + 8 * t + 8] for t in range(TILES)]
@@ -452,11 +474,21 @@
 
 
 def stars_kernel(
-    tiles, visits, uv_ref, off_ref, wd_ref, wc_ref, cnt_ref, tgt_ref, back_ref, star_ref, ccd_ref
+    tiles, visits, *refs
 ):
+    sources, (star_ref, ccd_ref), targets, sems = refs[:7], refs[7:9], refs[9:16], refs[16]
+    uv_ref, off_ref, wd_ref, wc_ref, cnt_ref, tgt_ref, back_ref = targets
+    copies = [
+        pltpu.make_async_copy(source, target, sems.at[at])
+        for at, (source, target) in enumerate(zip(sources, targets))
+    ]
+    for one in reversed(copies):
+        one.start()
+    for one in reversed(copies):
+        one.wait()
     back = back_ref[...]
     slots = back.shape[0]
-    ccd_ref[...] = back[:NCCD, AT_DET : AT_DET + 6]
+    ccd_ref[...] = back.T[AT_DET : AT_DET + 6, :NCCD]
     pieces = split3(back)
 
     def take(row):
@@ -502,12 +534,14 @@
     star_ref[pl.ds(1, tiles, stride=2), :] = inv_xy * grad_x + inv_yy * grad_y
 
 
-def plain(kernel, out_shape, scratch=()):
+def plain(kernel, out_shape, scratch=(), in_place=None):
+    extra = {} if in_place is None else {"in_specs": in_place}
     return pl.pallas_call(
         kernel,
         out_shape=out_shape,
+        **extra,
         scratch_shapes=list(scratch),
-        compiler_params=pltpu.CompilerParams(vmem_limit_bytes=48 * 1024 * 1024),
+        compiler_params=pltpu.CompilerParams(vmem_limit_bytes=64 * 1024 * 1024),
     )
 
 
@@ -526,13 +560,17 @@
     wd = w_diag.reshape(tiles * visits * 2, stars)
     wc = w_corr.transpose(1, 0, 2).reshape(tiles * visits, stars)
     cnt = star_count.reshape(1, tiles)
+    given = (uv, off, wd, wc, cnt, exposure_ids.T, ccd_ids.T, exp_slot.reshape(-1, LANES))
     out, tgt = plain(
         functools.partial(moments_kernel, tiles, visits, devices, cap, exp_local),
         (sds((slots, WIDTH), F32), sds((8, LANES), jnp.int32)),
-        (pltpu.VMEM((DEGREE + 1, stars, LANES), F32), pltpu.VMEM((8 * WIDTH, LANES), F32)),
-    )(uv, off, wd, wc, cnt, exposure_ids.T, ccd_ids.T, exp_slot.reshape(-1, LANES))
+        (pltpu.VMEM((DEGREE + 1, stars, LANES), F32), pltpu.VMEM((8 * WIDTH, LANES), F32))
+        + tuple(pltpu.VMEM(x.shape, x.dtype) for x in given)
+        + (pltpu.SemaphoreType.DMA((len(given),)),),
+        [HBM] * len(given),
+    )(*given)
+    tables = tuple(jnp.asarray(x) for x in expansion())
     recv = exchange(out.reshape(devices, cap, WIDTH), fields, shards_n, 0).reshape(slots, WIDTH)
-    top, low = expansion()
     exposure_update, back = plain(
         functools.partial(solve_kernel, cap),
         (sds((SIZE, exp_local), F32), sds((slots, LANES), F32)),
@@ -540,14 +578,21 @@
             pltpu.VMEM((8 * base_of(SIZE), exp_local), F32),
             pltpu.VMEM((8, SIZE, exp_local), F32),
             pltpu.VMEM((SIZE, exp_local), F32),
-        ),
-    )(recv, jnp.asarray(top), jnp.asarray(low))
+            pltpu.VMEM((slots, WIDTH), F32),
+        )
+        + tuple(pltpu.VMEM(x.shape, x.dtype) for x in tables)
+        + (pltpu.SemaphoreType.DMA((3,)),),
+        [HBM] * 3,
+    )(recv, *tables)
     got = exchange(back.reshape(devices, cap, LANES), fields, shards_n, 1).reshape(slots, LANES)
+    late = (*given[:5], tgt, got)
     star_update, ccd_update = plain(
         functools.partial(stars_kernel, tiles, visits),
-        (sds((tiles * 2, stars), F32), sds((NCCD, 6), F32)),
-    )(uv, off, wd, wc, cnt, tgt, got)
-    return star_update.reshape(tiles, 2, stars), exposure_update, ccd_update
+        (sds((tiles * 2, stars), F32), sds((6, NCCD), F32)),
+        tuple(pltpu.VMEM(x.shape, x.dtype) for x in late) + (pltpu.SemaphoreType.DMA((7,)),),
+        [HBM] * 7,
+    )(*late)
+    return star_update.reshape(tiles, 2, stars), exposure_update, ccd_update.T
 
 
 def solution(mesh):

time: 54.8 us -> 43.8 us (0.80)
  local copies, waits for them, and re-layouts: 12.7 us -> 0 us
  Pallas kernels: 40.8 us -> 43 us
    unnamed x39 -> x0, local copies, waits for them, and re-layouts: 12.7 us -> none
    pallas_call x2, Pallas kernels: 29.7 us -> 27.3 us  [exchange(): pl.pallas_call(functools.partial(exchange_kernel, fields, shards_n), out_...]
    pallas_call x1, Pallas kernels: 2.52 us -> 4.39 us  [shards(): plain(functools.partial(moments_kernel, tiles, visits, devices, cap, exp_...]
    pallas_call x1, Pallas kernels: 4.38 us -> 5.95 us  [shards(): plain(functools.partial(solve_kernel, cap), (sds((SIZE, exp_local), F32),...]
    pallas_call x1, Pallas kernels: 4.15 us -> 5.31 us  [shards(): plain(functools.partial(stars_kernel, tiles, visits), (sds((tiles * 2, st...]
where the time goes in v2:
time: 43.8 us; the launch traced here: 43.6 us
  Pallas kernels  43 us (98%)
  between operations  0.66 us (2%)
    pallas_call x2, Pallas kernels, exchange(): pl.pallas_call(functools.partial(exchange_kernel, fields, shards_n), out_...  27.3 us
    pallas_call x1, Pallas kernels, shards(): plain(functools.partial(solve_kernel, cap), (sds((SIZE, exp_local), F32),...  5.95 us
    pallas_call x1, Pallas kernels, shards(): plain(functools.partial(stars_kernel, tiles, visits), (sds((tiles * 2, st...  5.31 us
    pallas_call x1, Pallas kernels, shards(): plain(functools.partial(moments_kernel, tiles, visits, devices, cap, exp_...  4.39 us

profile of v2, /device:TPU:0, one launch (start us, length us, event | category | flops | bytes accessed | tf_op | source)
XLA Modules:
  0.0 43.6 jit_solution(17096951639026069469)
XLA Ops:
  0.6 4.4 %shard_map.121 = (f32[256,384]{1,0:T(8,128)}, s32[8,128]{1,0:T(8,128)}) custom-call(f32[192,128]{1,0:T(8,128)} %bitcast.19, f32[192,128]{1,0:T(8,128)} %bitcast.21, f32[192,128]{1,0:T(8,128)} %bitcast.23, f32[96,128]{1,0:T(8,128)} %bitcast.25, s32[1,16]{1,0:T(1,128)} %bitcast.31, s32[6,16]{1,0:T(8,128)} %bitcast.29, s32[6,16]{1,0:T(8,128)} %bitcast.30, ...), custom_call_target="tpu_custom_call" | custom-call | tf_op jit(solution)/shard_map/pallas_call | solution.py:564
  5.0 17.3 %shard_map.122 = f32[32,8,384]{2,1,0:T(8,128)} custom-call(f32[32,8,384]{2,1,0:T(8,128)} %bitcast.18), custom_call_target="tpu_custom_call" | custom-call | tf_op jit(solution)/shard_map/pallas_call | solution.py:320
  22.4 5.9 %shard_map.123 = (f32[56,128]{1,0:T(8,128)}, f32[256,128]{1,0:T(8,128)}) custom-call(f32[256,384]{1,0:T(8,128)} %bitcast.16, f32[1280,192]{1,0:T(8,128)} %constant.4.clone.top_any, f32[512,96]{1,0:T(8,128)} %constant.5.clone.low_any), custom_call_target="tpu_custom_call" | custom-call | tf_op jit(solution)/shard_map/pallas_call | solution.py:574
  28.3 10.0 %shard_map.124 = f32[32,8,128]{2,1,0:T(8,128)} custom-call(f32[32,8,128]{2,1,0:T(8,128)} %bitcast.27), custom_call_target="tpu_custom_call" | custom-call | tf_op jit(solution)/shard_map/pallas_call | solution.py:320
  38.3 5.3 %shard_map.125 = (f32[32,128]{1,0:T(8,128)}, f32[6,189]{1,0:T(8,128)}) custom-call(f32[192,128]{1,0:T(8,128)} %bitcast.20, f32[192,128]{1,0:T(8,128)} %bitcast.22, f32[192,128]{1,0:T(8,128)} %bitcast.24, f32[96,128]{1,0:T(8,128)} %bitcast.26, s32[1,16]{1,0:T(1,128)} %bitcast.32, s32[8,128]{1,0:T(8,128)} %get-tuple-element.9.refs_5_, f32[256,128]{1,0:T(8,128)} %bitcast.17), custom_call_target="tpu_custom_call" | custom-call | tf_op jit(solution)/shard_map/pallas_call | solution.py:589

commit v3 on v2

--- a/solution.py
+++ b/solution.py
@@ -273,11 +273,11 @@
     def greet(step, carry):
         peer = lax.rem(me + step, devices)
         pl.semaphore_signal(
-            barrier, inc=1, device_id=(peer // shards_n, peer % shards_n), device_id_type=MESH
+            barrier, inc=1, device_id=(lax.div(peer, shards_n), lax.rem(peer, shards_n)), device_id_type=MESH
         )
         return carry
 
-    lax.fori_loop(1, devices, greet, 0)
+    lax.fori_loop(1, devices, greet, 0, unroll=True)
     own = pltpu.make_async_copy(src_ref.at[me], dst_ref.at[me], own_sem)
     own.start()
     pl.semaphore_wait(barrier, devices - 1)
@@ -289,7 +289,7 @@
             dst_ref=dst_ref.at[me],
             send_sem=send_sem.at[step],
             recv_sem=recv_sem.at[step],
-            device_id=(peer // shards_n, peer % shards_n),
+            device_id=(lax.div(peer, shards_n), lax.rem(peer, shards_n)),
             device_id_type=MESH,
         )
 
@@ -305,13 +305,13 @@
             dst_ref=dst_ref.at[origin],
             send_sem=send_sem.at[step],
             recv_sem=recv_sem.at[step],
-            device_id=(origin // shards_n, origin % shards_n),
+            device_id=(lax.div(origin, shards_n), lax.rem(origin, shards_n)),
             device_id_type=MESH,
         ).wait_recv()
         return carry
 
-    lax.fori_loop(1, devices, launch, 0)
-    lax.fori_loop(1, devices, finish, 0)
+    lax.fori_loop(1, devices, launch, 0, unroll=True)
+    lax.fori_loop(1, devices, finish, 0, unroll=True)
     own.wait()
 
 

time: 43.8 us -> 43.7 us (level)
  no operation moved by 1% of the time
where the time goes in v3:
time: 43.7 us; the launch traced here: 43.5 us
  Pallas kernels  42.8 us (98%)
  between operations  0.66 us (2%)
    pallas_call x2, Pallas kernels, exchange(): pl.pallas_call(functools.partial(exchange_kernel, fields, shards_n), out_...  27.2 us
    pallas_call x1, Pallas kernels, shards(): plain(functools.partial(solve_kernel, cap), (sds((SIZE, exp_local), F32),...  5.94 us
    pallas_call x1, Pallas kernels, shards(): plain(functools.partial(stars_kernel, tiles, visits), (sds((tiles * 2, st...  5.31 us
    pallas_call x1, Pallas kernels, shards(): plain(functools.partial(moments_kernel, tiles, visits, devices, cap, exp_...  4.39 us

profile of v3, /device:TPU:0, one launch (start us, length us, event | category | flops | bytes accessed | tf_op | source)
XLA Modules:
  0.0 43.5 jit_solution(2871268770707836093)
XLA Ops:
  0.6 4.4 %shard_map.121 = (f32[256,384]{1,0:T(8,128)}, s32[8,128]{1,0:T(8,128)}) custom-call(f32[192,128]{1,0:T(8,128)} %bitcast.19, f32[192,128]{1,0:T(8,128)} %bitcast.21, f32[192,128]{1,0:T(8,128)} %bitcast.23, f32[96,128]{1,0:T(8,128)} %bitcast.25, s32[1,16]{1,0:T(1,128)} %bitcast.31, s32[6,16]{1,0:T(8,128)} %bitcast.29, s32[6,16]{1,0:T(8,128)} %bitcast.30, ...), custom_call_target="tpu_custom_call" | custom-call | tf_op jit(solution)/shard_map/pallas_call | solution.py:564
  5.0 17.2 %shard_map.122 = f32[32,8,384]{2,1,0:T(8,128)} custom-call(f32[32,8,384]{2,1,0:T(8,128)} %bitcast.18), custom_call_target="tpu_custom_call" | custom-call | tf_op jit(solution)/shard_map/pallas_call | solution.py:320
  22.3 5.9 %shard_map.123 = (f32[56,128]{1,0:T(8,128)}, f32[256,128]{1,0:T(8,128)}) custom-call(f32[256,384]{1,0:T(8,128)} %bitcast.16, f32[1280,192]{1,0:T(8,128)} %constant.4.clone.top_any, f32[512,96]{1,0:T(8,128)} %constant.5.clone.low_any), custom_call_target="tpu_custom_call" | custom-call | tf_op jit(solution)/shard_map/pallas_call | solution.py:574
  28.2 9.9 %shard_map.124 = f32[32,8,128]{2,1,0:T(8,128)} custom-call(f32[32,8,128]{2,1,0:T(8,128)} %bitcast.27), custom_call_target="tpu_custom_call" | custom-call | tf_op jit(solution)/shard_map/pallas_call | solution.py:320
  38.2 5.3 %shard_map.125 = (f32[32,128]{1,0:T(8,128)}, f32[6,189]{1,0:T(8,128)}) custom-call(f32[192,128]{1,0:T(8,128)} %bitcast.20, f32[192,128]{1,0:T(8,128)} %bitcast.22, f32[192,128]{1,0:T(8,128)} %bitcast.24, f32[96,128]{1,0:T(8,128)} %bitcast.26, s32[1,16]{1,0:T(1,128)} %bitcast.32, s32[8,128]{1,0:T(8,128)} %get-tuple-element.9.refs_5_, f32[256,128]{1,0:T(8,128)} %bitcast.17), custom_call_target="tpu_custom_call" | custom-call | tf_op jit(solution)/shard_map/pallas_call | solution.py:589
